TPU v7x, 32 devices: a whole 2x2x4 slice. The times are simulated.
32 devices in a mesh: dp: 16 (over z, x, core), pair: 2 (over y).
Axes of the slice: x: 2, y: 2, z: 4, core: 2. Of those that a mesh axis runs over, the one named last changes fastest.
Arguments:
- tokens: bfloat16 [2, 4096, 768], P('pair', 'dp'), may hold values from -6 to 6
- cotangent: bfloat16 [2, 4096, 768], P('pair', 'dp'), may hold values from -6 to 6
- lengths: int32 [2, 16, 2], P('pair', 'dp'), may hold values from 1 to 192, 256 in all within a row
- mats: float32 [2, 7077888], P(None, ('dp', 'pair')), may hold values from -1.6329932 to 1.6329932, as said below
- mats_m: float32 [2, 7077888], P(None, ('dp', 'pair')), may hold values from -0.5 to 0.5
- mats_v: float32 [2, 7077888], P(None, ('dp', 'pair')), may hold values from 0.0005 to 0.008
- vecs: float32 [2, 9216], P(None, ('dp', 'pair')), may hold values from -1.2 to 2.2, as said below
- vecs_m: float32 [2, 9216], P(None, ('dp', 'pair')), may hold values from -0.5 to 0.5
- vecs_v: float32 [2, 9216], P(None, ('dp', 'pair')), may hold values from 0.0005 to 0.008
Outputs:
- head_out: bfloat16 [2, 4096, 768], P('pair', 'dp')
- token_grad: float32 [2, 4096, 768], P('pair', 'dp')
- contrastive: float32 [], replicated
- grad_norm: float32 [], replicated
- new_mats: float32 [2, 7077888], P(None, ('dp', 'pair'))
- new_mats_m: float32 [2, 7077888], P(None, ('dp', 'pair'))
- new_mats_v: float32 [2, 7077888], P(None, ('dp', 'pair'))
- new_vecs: float32 [2, 9216], P(None, ('dp', 'pair'))
- new_vecs_m: float32 [2, 9216], P(None, ('dp', 'pair'))
- new_vecs_v: float32 [2, 9216], P(None, ('dp', 'pair'))
Inputs may be any that keep to these rules, and one draw needn't show every extreme that they name: Each row of 2 lengths sums to 256; its longest span has at most 192 tokens. `mats`: Real-valued entries. `vecs`: Real-valued entries.
All inputs are finite; a program needn't handle non-finite values.
Results may differ from a plain program's by a relative error of at most 0.017.
Values may be sent and summed in bfloat16 or wider, within the bound.
No kernel may reach another device: no remote copies, remote signals or barrier semaphores. Data moves between devices by JAX's collectives and lax.ppermute only.
A program may use at most 256 MiB of HBM per device.

v0:
```python
import math

import jax
import jax.numpy as jnp
from jax import lax
from jax.experimental import pallas as pl
from jax.experimental.pallas import tpu as pltpu
from jax.sharding import PartitionSpec as P

D = 768
HEADS = 12
HEAD_DIM = 64
FF = 3072
STEP = 10
PL = 7077888
QL = 9216

norm_epsilon = 1e-12
masked_score = -1000000000.0
beta_one = 0.9
beta_two = 0.999
adam_epsilon = 1e-08
weight_decay = 0.01

F32 = jnp.float32
BF16 = jnp.bfloat16
TOK = 256
GRAN = 96
GRANS = PL // D // GRAN
VMEM_BYTES = 63_000_000

V_BQ, V_BV, V_BO, V_G1, V_C1, V_B1, V_B2, V_G2, V_C2 = 0, 1, 2, 3, 4, 5, 9, 10, 11

R_E, R_DF, R_H, R_DA, R_ATT, R_DO, R_U, R_DQ, R_Q, R_DATT, R_WK, R_PU, R_VEC = (
    0, 8, 10, 12, 20, 22, 24, 26, 28, 30, 32, 56, 80,
)
PAY = 96


def nn(a, b):
    return lax.dot_general(a, b, (((1,), (0,)), ((), ())), preferred_element_type=F32)


def nt(a, b):
    return lax.dot_general(a, b, (((1,), (1,)), ((), ())), preferred_element_type=F32)


def tn(a, b):
    return lax.dot_general(a, b, (((0,), (0,)), ((), ())), preferred_element_type=F32)


def iota(shape, axis):
    return lax.broadcasted_iota(jnp.int32, shape, axis)


def erf(x):
    x = jnp.clip(x, -3.832506856900711, 3.832506856900711)
    s = x * x
    top = 0.00022905065861350646
    for c in (0.0034082910107109506, 0.050955695062380861, 0.18520832239976145, 1.128379143519084):
        top = top * s + c
    low = -1.1791602954361697e-7
    for c in (
        0.000023547966471313185,
        0.0010179625278914885,
        0.014070470171167667,
        0.11098505178285362,
        0.49746925110067538,
        1.0,
    ):
        low = low * s + c
    return x * top / low


def gelu_both(a):
    phi = 0.5 + 0.5 * erf(a * math.sqrt(0.5))
    return a * phi, phi + a * jnp.exp(-0.5 * a * a) * (1.0 / math.sqrt(2.0 * math.pi))


def norm_forward(r):
    centred = r - jnp.mean(r, axis=-1, keepdims=True)
    rstd = lax.rsqrt(jnp.mean(centred * centred, axis=-1, keepdims=True) + norm_epsilon)
    return centred * rstd, rstd


def norm_backward(dy, gain, xhat, rstd):
    dx = dy * gain
    return rstd * (
        dx - jnp.mean(dx, axis=-1, keepdims=True) - xhat * jnp.mean(dx * xhat, axis=-1, keepdims=True)
    )


def colsum(v):
    return jnp.sum(v, axis=0, keepdims=True)


def flip(v, axis, bit):
    return lax.ppermute(v, axis, [(i, i ^ bit) for i in range(lax.axis_size(axis))])


def core_flip(v):
    return flip(v, "dp", 1)


def x_flip(v):
    return flip(v, "dp", 2)


def y_flip(v):
    return flip(v, "pair", 1)


def z_up(v):
    n = lax.axis_size("dp")
    return lax.ppermute(v, "dp", [(i, (i + 4) % n) for i in range(n)])


def z_turn(v, places):
    n = lax.axis_size("dp")
    return lax.ppermute(v, "dp", [(i, (i + 4 * places) % n) for i in range(n)])


def xor_flip(v, pair_bit, dp_bits):
    if not pair_bit:
        return flip(v, "dp", dp_bits)
    n = lax.axis_size("dp")
    return lax.ppermute(v, ("dp", "pair"), [(i, i ^ (2 * dp_bits + 1)) for i in range(2 * n)])


def fence(values):
    return list(lax.optimization_barrier(tuple(values)))


SMALL_STEPS = (((1, 0), (0, 1), (1, 1)), ((0, 2), (0, 4), (0, 6)), ((0, 8),))


def gather_step(v, step, device):
    got = [v] + [xor_flip(v, *bits) for bits in SMALL_STEPS[step]]
    here = (device >> (2 * step)) & (len(got) - 1)
    return lambda: jnp.concatenate([pick(here ^ p, got) for p in range(len(got))], 0)


SUM_STEPS = (((0, 1),), ((1, 0), (0, 2), (1, 2)), ((0, 4), (0, 8), (0, 12)))


def sum_quick(v):
    for bits in SUM_STEPS:
        got = [v] + [xor_flip(v, *b) for b in bits]
        v = got[0] + got[1] if len(got) == 2 else (got[0] + got[1]) + (got[2] + got[3])
    return v


def pick(index, cases):
    return lax.select_n(index, *cases)


GATHER_ROUNDS = (
    ("x0", "y0", "s1"),
    ("d0", "e0", "x1", "y1", "s2"),
    ("d1", "e1", "x2", "y2", "s3"),
    ("d2", "e2", "x3", "y3"),
    ("d3", "e3"),
)


SEND_VEC, SEND_ONE, SEND = 288, 304, 592


def gather_blocks(own):
    have = {"s0": own}
    across = ["s0"]
    for r, tasks in enumerate(GATHER_ROUNDS):
        sources = {}
        for name in tasks:
            kind, k = name[0], int(name[1])
            sources[name] = {"s": f"s{k - 1}", "x": f"s{k}", "y": f"s{k}", "d": f"x{k}", "e": f"y{k}"}[kind]
        names = list(dict.fromkeys([*sources.values(), *across]))
        if r:
            have.update(zip(names, fence([have[i] for i in names])))
        for name, source in sources.items():
            move = {
                "s": z_up, "x": x_flip, "y": y_flip, "d": lambda v: y_flip(v[:SEND_ONE]), "e": lambda v: x_flip(v[SEND_ONE:])
            }[name[0]]
            have[name] = move(have[source])
        if 0 < r < 4:
            names = [*across, *tasks[:2]]
            have.update(zip(names, fence([have[i] for i in names])))
        for i in across:
            have["c" + i] = core_flip(have[i])
        across = list(tasks)
    for i in across:
        have["c" + i] = core_flip(have[i])
    return [[have[c + kind + str(k)] for c in ("", "c") for k in range(4) for kind in kinds] for kinds in ("sxyd", "sxye")]


def add16(a, b):
    return (a.astype(F32) + b.astype(F32)).astype(BF16)


GROUPS = ((3, 2), (1, 0))
GROUP_ROWS = 2304
HALF = 1152
SX, SY, QX, QY, OWN = 0, 576, 1152, 1440, 1728


def by_kind(granule, emit):
    joint = granule < 24
    wide = (granule >= 32) & (granule < 64)
    pl.when(joint)(lambda: emit(3))
    pl.when(wide)(lambda: emit(4))
    pl.when(jnp.logical_not(joint | wide))(lambda: emit(1))


def pack_kernel(info, flat, vecs, out):
    out[SEND_VEC:SEND_ONE, :] = jnp.zeros((SEND_ONE - SEND_VEC, D), BF16)
    both = vecs[...]
    out[SEND_VEC:SEND_ONE, 0:288] = jnp.concatenate([both, jnp.zeros((14, 288), F32)], 0).astype(BF16)
    for gi in range(3):

        def emit(n, gi=gi):
            m = GRAN // n
            for layer in range(2):
                for j in range(6):
                    parts = [
                        flat[pl.ds(12 * (GRAN * gi + p) + 2 * j + layer, m, stride=12 * n), :] for p in range(n)
                    ]
                    tile = parts[0] if n == 1 else jnp.concatenate(parts, 0)
                    at = SEND_ONE * layer + GRAN * gi
                    out[at : at + GRAN, 128 * j : 128 * (j + 1)] = tile.astype(BF16)

        by_kind(3 * info[0] + gi, emit)


def owner(info, plane, kind, other):
    return (
        8 * plane
        + 4 * jnp.bitwise_xor(info[2], kind & 1)
        + 2 * jnp.bitwise_xor(info[3], other)
        + jnp.bitwise_xor(info[4], kind >> 1)
    )


def fill(info, pieces, diagonals, block, wbuf, vbuf, sem):
    vecs = []
    for other in (0, 1):
        for k in range(4):
            for kind in range(4):
                i = 16 * other + 4 * k + kind
                source = (pieces if kind < 3 else diagonals)[i].at[pl.ds(SEND_VEC, 16)]
                dev = owner(info, (info[1] + 4 - k) & 3, kind, other)
                vecs.append(pltpu.make_async_copy(source, vbuf.at[dev], sem.at[32 + i]))
    for copy in vecs:
        copy.start()

    def copies(plane, k):
        made = []
        for other in (0, 1):
            for kind in range(4):
                source = pieces[16 * other + 4 * k + kind].at[pl.ds(SEND_ONE if block and kind < 3 else 0, 288)]
                rows = pl.ds(pl.multiple_of(288 * owner(info, plane, kind, other), 16), 288)
                made.append(pltpu.make_async_copy(source, wbuf.at[rows], sem.at[8 * plane + 2 * kind + other]))
        return made

    for plane in range(4):
        for k in range(4):

            @pl.when(((info[1] + 4 - plane) & 3) == k)
            def _(plane=plane, k=k):
                for copy in copies(plane, k):
                    copy.start()

    def wait_vecs():
        for copy in vecs:
            copy.wait()

    def wait(plane):
        for copy in copies(plane, 0):
            copy.wait()

    return wait_vecs, wait


def order_vec(vbuf, block, vec):
    every = vbuf[:, 0:2, :].astype(F32)
    for q in range(QL // GRAN):
        to, lo = GRAN * (q % 8), GRAN * (q % 3)
        vec[q // 8 : q // 8 + 1, to : to + GRAN] = every[q // 3, block : block + 1, lo : lo + GRAN]


def split_w1(wbuf, w1):
    def step(i, carry):
        rows = wbuf[pl.ds(32 + 4 * i, 4)].astype(F32)
        for j in range(4):
            part = rows[:, 24 * j : 24 * (j + 1), :].reshape(GRAN, D).astype(BF16)
            w1[j, pl.ds(pl.multiple_of(GRAN * i, GRAN), GRAN), :] = part
        return carry

    lax.fori_loop(0, 8, step, 0)


def w_in(wbuf, j):
    return wbuf[0:24, 32 * j : 32 * (j + 1), :].reshape(D, D)


def w_out(wbuf):
    return wbuf[24:32].reshape(D, D)


def w_shrink(wbuf, j):
    return wbuf[64 + 8 * j : 72 + 8 * j].reshape(D, D)


def expander():
    r, c = iota((32, 16), 0), iota((32, 16), 1)
    return ((r < 24) & ((r & 1) == c)).astype(BF16)


def head_mask():
    r, lane = iota((32, D), 0), iota((32, D), 1)
    return (r < 24) & ((r >> 1) == (lane >> 6))


def spread(expand, mask, rows):
    return jnp.where(mask, nn(expand, rows), 0.0).astype(BF16)


def first_forward(
    info, u_ref, *refs
):
    pieces = diagonals = refs[:32]
    y_out, xh1_o, rs1_o, xh2_o, rs2_o, gp_o, e_o, h_o, att_o, u_o, q_o, pu_o, qk_o, p_o, vec, vbuf, wflat, w1, sem = refs[32:]
    wait_vecs, wait = fill(info, pieces, diagonals, 0, wflat, vbuf, sem)
    wbuf = wflat.reshape(GRANS, GRAN, D)
    start = info[5]
    u = u_ref[...]
    r, t = iota((16, TOK), 0), iota((16, TOK), 1)
    picker = (((r == 0) & (t == 0)) | ((r == 1) & (t == start))).astype(BF16)
    cls = nn(picker, u)
    cls16 = cls.astype(BF16)
    expand, mask = expander(), head_mask()
    r, t = iota((32, TOK), 0), iota((32, TOK), 1)
    inside = (t >= start).astype(jnp.int32) == (r & 1)
    real = r < 24
    wait_vecs()
    order_vec(vbuf, 0, vec)
    wait(0)
    q = (nn(cls16, w_in(wbuf, 0)) + vec[V_BQ : V_BQ + 1, :]).astype(BF16)
    qk = nt(spread(expand, mask, q), w_in(wbuf, 1)).astype(BF16)
    scores = jnp.where(inside, nt(qk, u) * HEAD_DIM**-0.5, masked_score)
    raised = jnp.exp(scores - jnp.max(scores, axis=-1, keepdims=True))
    portions = jnp.where(real, raised / jnp.sum(raised, axis=-1, keepdims=True), 0.0)
    low = portions.astype(BF16)
    pu = nn(low, u).astype(BF16)
    weight = jnp.sum(low.astype(F32), axis=-1, keepdims=True)
    heads = nn(pu, w_in(wbuf, 2)) + weight * vec[V_BV : V_BV + 1, :]
    att = tn(expand, jnp.where(mask, heads, 0.0).astype(BF16)).astype(BF16)
    wait(1)
    xhat, rstd = norm_forward(cls + nn(att, w_out(wbuf)) + vec[V_BO : V_BO + 1, :])
    xh1_o[...] = xhat
    rs1_o[...] = jnp.broadcast_to(rstd, (16, 128))
    h = xhat * vec[V_G1 : V_G1 + 1, :] + vec[V_C1 : V_C1 + 1, :]
    h16 = h.astype(BF16)
    f = vec[V_B2 : V_B2 + 1, :]
    wait(2)
    split_w1(wbuf, w1)
    wait(3)
    for j in range(4):
        e, gp = gelu_both(nn(h16, w1[j]) + vec[V_B1 + j : V_B1 + j + 1, :])
        e = e.astype(BF16)
        e_o[j] = e
        gp_o[j] = gp
        f = f + nn(e, w_shrink(wbuf, j))
    xhat, rstd = norm_forward(h + f)
    xh2_o[...] = xhat
    rs2_o[...] = jnp.broadcast_to(rstd, (16, 128))
    y_out[...] = xhat * vec[V_G2 : V_G2 + 1, :] + vec[V_C2 : V_C2 + 1, :]
    h_o[...] = h16
    att_o[...] = att
    u_o[...] = cls16
    q_o[...] = q
    pu_o[...] = pu
    qk_o[...] = qk
    p_o[...] = portions


def first_backward(
    info, u_ref, cls_all, dz, vg1, xh1, rs1, xh2, rs2, gp_i, e_i, h_i, att_i, ucls, q_i, pu_i, qk_i, p_i, *refs
):
    pieces = diagonals = refs[:32]
    tg_out, pay_out, loss_out, vec, vbuf, wflat, w1, rows16, dcls, pay, sem = refs[32:]
    wait_vecs, wait = fill(info, pieces, diagonals, 0, wflat, vbuf, sem)
    wbuf = wflat.reshape(GRANS, GRAN, D)
    start = info[5]
    u = u_ref[...]
    keys = cls_all[...]
    n_keys = keys.shape[0]
    scale = 2.0 / math.sqrt(D)
    r, c = iota((n_keys, n_keys), 0), iota((n_keys, n_keys), 1)
    scores = jnp.where(r == c, masked_score, nt(keys, keys) * scale)
    top = jnp.max(scores, axis=-1, keepdims=True)
    raised = jnp.exp(scores - top)
    total = jnp.sum(raised, axis=-1, keepdims=True)
    partner = jnp.bitwise_xor(r, 2) == c
    positive = jnp.sum(jnp.where(partner, scores, 0.0), axis=-1, keepdims=True)
    terms = top + jnp.log(total) - positive
    loss_out[0, 0] = jnp.sum(terms) * (1.0 / n_keys)
    pull = (raised / total - partner.astype(F32)).astype(BF16)
    dcls[...] = (nn(pull, keys) + tn(pull, keys)) * scale
    rows16[...] = jnp.zeros((16, D), F32)
    rows16[0:1, :] = dz[0:1, :] + dcls[pl.ds(2 * info[0], 1), :]
    rows16[1:2, :] = dz[pl.ds(start, 1), :] + dcls[pl.ds(2 * info[0] + 1, 1), :]
    dy = rows16[...]
    wait_vecs()
    order_vec(vbuf, 0, vec)
    for plane in range(4):
        wait(plane)
    split_w1(wbuf, w1)
    xhat = xh2[...]
    pay[R_VEC + 14 : R_VEC + 15, :] = colsum(dy * xhat)
    pay[R_VEC + 15 : R_VEC + 16, :] = colsum(dy)
    dr2 = norm_backward(dy, vec[V_G2 : V_G2 + 1, :], xhat, rs2[:, 0:1])
    df = dr2.astype(BF16)
    pay[R_DF : R_DF + 2, :] = df.astype(F32)[0:2, :]
    dh = dr2
    for j in range(4):
        da = (gp_i[j] * nt(df, w_shrink(wbuf, j))).astype(BF16)
        pay[R_E + 2 * j : R_E + 2 * j + 2, :] = e_i[j].astype(F32)[0:2, :]
        pay[R_DA + 2 * j : R_DA + 2 * j + 2, :] = da.astype(F32)[0:2, :]
        dh = dh + nt(da, w1[j])
    xhat = xh1[...]
    pay[R_VEC + 12 : R_VEC + 13, :] = colsum(dh * xhat)
    pay[R_VEC + 13 : R_VEC + 14, :] = colsum(dh)
    dr1 = norm_backward(dh, vec[V_G1 : V_G1 + 1, :], xhat, rs1[:, 0:1])
    do = dr1.astype(BF16)
    datt = nt(do, w_out(wbuf)).astype(BF16)
    expand, mask = expander(), head_mask()
    portions = p_i[...]
    low = portions.astype(BF16)
    each = spread(expand, mask, datt)
    dvk = nt(each, w_in(wbuf, 2)).astype(BF16)
    constant = jnp.sum(each.astype(F32) * vec[V_BV : V_BV + 1, :], axis=-1, keepdims=True)
    dp = nt(dvk, u) + constant
    ds = (portions * (dp - jnp.sum(dp * portions, axis=-1, keepdims=True))).astype(BF16)
    dsu = nn(ds, u)
    part = jnp.where(mask, nn(dsu.astype(BF16), w_in(wbuf, 1)) * HEAD_DIM**-0.5, 0.0).astype(BF16)
    dq = tn(expand, part).astype(BF16)
    rows16[...] = dr1 + nt(dq, w_in(wbuf, 0))
    du = tn(ds, qk_i[...]) * HEAD_DIM**-0.5 + tn(low, dvk)
    is_cls = (iota((TOK, 1), 0) == 0) | (iota((TOK, 1), 0) == start)
    tg_out[...] = du + jnp.where(is_cls, 0.0, dz[...])
    tg_out[0:1, :] = tg_out[0:1, :] + rows16[0:1, :]
    tg_out[pl.ds(start, 1), :] = tg_out[pl.ds(start, 1), :] + rows16[1:2, :]
    for row, rows in ((R_H, h_i), (R_ATT, att_i), (R_U, ucls), (R_Q, q_i)):
        pay[row : row + 2, :] = rows[...].astype(F32)[0:2, :]
    for row, rows in ((R_DO, do), (R_DQ, dq), (R_DATT, datt)):
        pay[row : row + 2, :] = rows.astype(F32)[0:2, :]
    pay[R_WK : R_WK + 24, :] = dsu[0:24, :] * HEAD_DIM**-0.5
    pay[R_PU : R_PU + 24, :] = pu_i[...].astype(F32)[0:24, :]
    pay[R_VEC : R_VEC + 12, :] = vg1[0:12, :]
    pay_out[...] = pay[...].astype(BF16)


def lanes(p):
    return pl.ds(pl.multiple_of(128 * p, 128), 128)


def send_groups(info, grads, planes, outs, sem):
    sends = []
    for other in (1, 0):
        for i, t in enumerate(planes):
            for kind, parts in ((3, ((SY + 144 * i, 0), (SX + 144 * i, 144))),
                                (1, ((QX + 144 * i, 0), (SX + 288 + 144 * i, 144))),
                                (2, ((SY + 288 + 144 * i, 0), (QY + 144 * i, 144))),
                                (0, ((OWN + 288 * i, 0),))):
                dev = owner(info, t, kind, other)
                rows = 288 if kind == 0 else 144
                for to, lo in parts:
                    source = grads.at[pl.ds(pl.multiple_of(288 * dev + lo, 16), rows)]
                    sends.append(pltpu.make_async_copy(source, outs[1 - other][to // HALF].at[pl.ds(to % HALF, rows)], sem.at[len(sends)]))
                    sends[-1].start()
    return sends


def second_block(info, u_ref, cot_ref, y_ref, *refs):
    pieces = refs[:32]
    diagonals = {4 * i + 3: refs[32 + i] for i in range(8)}
    head_out, dr_out, vg_out, zb, qs, ks, vs, att = refs[40:48]
    pm_out, w1_grad, theirs1, theirs2, mine1, mine2 = refs[48:54]
    (vec, vbuf, wflat, w1, grads, zf, pm, xh1, hb, ht, gp, es, das, xh2, acc, stage, dfs, sem, osem) = refs[54:]
    wait_vecs, wait = fill(info, pieces, diagonals, 1, wflat, vbuf, sem)
    wbuf = wflat.reshape(GRANS, GRAN, D)
    gbuf = grads.reshape(GRANS, GRAN, D)
    start = info[5]
    zf[...] = u_ref[...].astype(F32)
    zf[0:1, :] = y_ref[0:1, :]
    zf[pl.ds(start, 1), :] = y_ref[1:2, :]
    z16 = zf[...].astype(BF16)
    zb[...] = z16
    wait_vecs()
    order_vec(vbuf, 1, vec)
    wait(0)
    qs[...] = (nn(z16, w_in(wbuf, 0)) + vec[V_BQ : V_BQ + 1, :]).astype(BF16)
    ks[...] = nn(z16, w_in(wbuf, 1)).astype(BF16)
    vs[...] = (nn(z16, w_in(wbuf, 2)) + vec[V_BV : V_BV + 1, :]).astype(BF16)
    low_lane = iota((TOK, 128), 1) < HEAD_DIM
    same = (iota((TOK, TOK), 0) >= start) == (iota((TOK, TOK), 1) >= start)

    def attend(p, carry):
        qp, kp, vp = qs[:, lanes(p)], ks[:, lanes(p)], vs[:, lanes(p)]
        res = []
        for hh in range(2):
            qm = jnp.where(low_lane == (hh == 0), qp, jnp.zeros_like(qp))
            s = jnp.where(same, nt(qm, kp) * HEAD_DIM**-0.5, masked_score)
            raised = jnp.exp(s - jnp.max(s, axis=-1, keepdims=True))
            portions = raised / jnp.sum(raised, axis=-1, keepdims=True)
            pm[2 * p + hh] = portions
            res.append(nn(portions.astype(BF16), vp))
        att[:, lanes(p)] = jnp.where(low_lane, res[0], res[1]).astype(BF16)
        return carry

    lax.fori_loop(0, 6, attend, 0, unroll=True)
    saved = [pltpu.make_async_copy(pm, pm_out, osem.at[28])]
    saved[0].start()
    wait(1)
    xhat, rstd1 = norm_forward(zf[...] + (nn(att[...], w_out(wbuf)) + vec[V_BO : V_BO + 1, :]))
    xh1[...] = xhat
    h = xhat * vec[V_G1 : V_G1 + 1, :] + vec[V_C1 : V_C1 + 1, :]
    hb[...] = h.astype(BF16)
    ht[...] = h.T.astype(BF16)
    acc[...] = h + vec[V_B2 : V_B2 + 1, :]
    wait(2)
    split_w1(wbuf, w1)
    wait(3)
    for j in range(4):
        e, slope = gelu_both(nn(hb[...], w1[j]) + vec[V_B1 + j : V_B1 + j + 1, :])
        gp[j] = slope
        e = e.astype(BF16)
        es[j] = e
        acc[...] += nn(e, w_shrink(wbuf, j))
    xhat, rstd2 = norm_forward(acc[...])
    xh2[...] = xhat
    head_out[...] = (xhat * vec[V_G2 : V_G2 + 1, :] + vec[V_C2 : V_C2 + 1, :]).astype(BF16)

    vg_out[...] = jnp.zeros((16, D), F32)
    dy = cot_ref[...].astype(F32)
    vg_out[V_G2 : V_G2 + 1, :] = colsum(dy * xh2[...])
    vg_out[V_C2 : V_C2 + 1, :] = colsum(dy)
    dr = norm_backward(dy, vec[V_G2 : V_G2 + 1, :], xh2[...], rstd2)
    acc[...] = dr
    df = dr.astype(BF16)
    dfs[...] = df
    vg_out[V_B2 : V_B2 + 1, :] = colsum(df.astype(F32))
    for j in range(4):
        df = dfs[...]
        gbuf[64 + 8 * j : 72 + 8 * j] = tn(es[j], df).astype(BF16).reshape(8, GRAN, D)
        da = (gp[j] * nt(df, w_shrink(wbuf, j))).astype(BF16)
        das[j] = da
        vg_out[V_B1 + j : V_B1 + j + 1, :] = colsum(da.astype(F32))

    def expand_grad(i, carry):
        rows = ht[pl.ds(pl.multiple_of(192 * i, 192), 192), :]
        for j in range(4):
            stage[:, 24 * j : 24 * (j + 1), :] = nn(rows, das[j]).reshape(8, 24, D)
        gbuf[pl.ds(32 + 8 * i, 8)] = stage[...].astype(BF16)
        return carry

    lax.fori_loop(2, 4, expand_grad, 0)
    saved += send_groups(info, grads, GROUPS[0], ((theirs1, theirs2), (mine1, mine2)), osem)
    lax.fori_loop(0, 2, expand_grad, 0)
    saved.append(pltpu.make_async_copy(grads.at[pl.ds(3072, 1536)], w1_grad, osem.at[29]))
    saved[-1].start()
    for j in range(4):
        acc[...] += nt(das[j], w1[j])
    dh = acc[...]
    vg_out[V_G1 : V_G1 + 1, :] = colsum(dh * xh1[...])
    vg_out[V_C1 : V_C1 + 1, :] = colsum(dh)
    dr_out[...] = norm_backward(dh, vec[V_G1 : V_G1 + 1, :], xh1[...], rstd1)
    for copy in saved:
        copy.wait()


def second_attention(info, dr, vg_in, zb, qs, ks, vs, att, *refs):
    pieces = refs[:32]
    pm_in, w1_grad, dz_out, vg_out, theirs1, theirs2, mine1, mine2, wflat, grads, pm, datt, dqs, dks, dvs, sem = refs[32:]
    wbuf = wflat.reshape(GRANS // 2, GRAN, D)
    gbuf = grads.reshape(GRANS // 2, GRAN, D)
    waits = []
    for other in (0, 1):
        for k in range(4):
            for kind in range(4):
                i = 16 * other + 4 * k + kind
                dev = owner(info, (info[1] + 4 - k) & 3, kind, other)
                source = pieces[i].at[pl.ds(SEND_ONE if kind < 3 else 0, 288)]
                rows = pl.ds(pl.multiple_of(288 * jnp.minimum(dev, 15), 16), 288)
                copy = pltpu.make_async_copy(source, wflat.at[rows], sem.at[i])
                used = dev < 11
                pl.when(used)(copy.start)
                waits.append((used, copy))
    saved = [
        pltpu.make_async_copy(pm_in, pm, sem.at[32]),
        pltpu.make_async_copy(w1_grad, grads.at[pl.ds(3072, 1536)], sem.at[33]),
    ]
    for copy in saved:
        copy.start()
    vg_out[...] = vg_in[...]
    do = dr[...].astype(BF16)
    vg_out[V_BO : V_BO + 1, :] = colsum(do.astype(F32))
    gbuf[24:32] = tn(att[...], do).astype(BF16).reshape(8, GRAN, D)
    for used, copy in waits:
        pl.when(used)(copy.wait)
    datt[...] = nt(do, w_out(wbuf)).astype(BF16)
    saved[0].wait()
    low_lane = iota((TOK, 128), 1) < HEAD_DIM

    def attend_back(p, carry):
        qp, kp, vp, dp_ = qs[:, lanes(p)], ks[:, lanes(p)], vs[:, lanes(p)], datt[:, lanes(p)]
        dq, dk, dv = [], [], []
        for hh in range(2):
            portions = pm[2 * p + hh]
            dam = jnp.where(low_lane == (hh == 0), dp_, jnp.zeros_like(dp_))
            dp = nt(dam, vp)
            dv.append(tn(portions.astype(BF16), dp_))
            ds = (portions * (dp - jnp.sum(dp * portions, axis=-1, keepdims=True))).astype(BF16)
            dq.append(nn(ds, kp))
            dk.append(tn(ds, qp))
        dqs[:, lanes(p)] = (jnp.where(low_lane, dq[0], dq[1]) * HEAD_DIM**-0.5).astype(BF16)
        dks[:, lanes(p)] = (jnp.where(low_lane, dk[0], dk[1]) * HEAD_DIM**-0.5).astype(BF16)
        dvs[:, lanes(p)] = jnp.where(low_lane, dv[0], dv[1]).astype(BF16)
        return carry

    lax.fori_loop(0, 6, attend_back, 0, unroll=True)
    vg_out[V_BQ : V_BQ + 1, :] = colsum(dqs[...].astype(F32))
    vg_out[V_BV : V_BV + 1, :] = colsum(dvs[...].astype(F32))
    dz = dr[...]
    for j, part in enumerate((dqs, dks, dvs)):
        gbuf[0:24, 32 * j : 32 * (j + 1), :] = tn(zb[...], part[...]).astype(BF16).reshape(24, 32, D)
    saved[1].wait()
    sends = send_groups(info, grads, GROUPS[1], ((theirs1, theirs2), (mine1, mine2)), sem)
    for j, part in enumerate((dqs, dks, dvs)):
        dz = dz + nt(part[...], w_in(wbuf, j))
    dz_out[...] = dz
    for copy in sends:
        copy.wait()


def total_kernel(mine, came, over_x, over_y, last_x, last_y, first, second):
    for i, out in enumerate((first, second)):
        part = slice(144 * i, 144 * (i + 1))
        for half, (one, two) in enumerate(((last_x, over_y), (over_x, last_y))):
            own = slice(288 * i + 144 * half, 288 * i + 144 * (half + 1))
            both = mine[own, :].astype(F32) + came[own, :].astype(F32)
            out[144 * half : 144 * (half + 1), :] = (
                both + one[part, :].astype(F32) + two[part, :].astype(F32)
            ).astype(BF16)


def owner_grad(info, *refs):
    pieces = refs[:10]
    out, vec_out, pbuf, abuf, qbuf, sem = refs[10:]
    copies = []
    at = 0
    for i, piece in enumerate(pieces):
        copies.append(pltpu.make_async_copy(piece, pbuf.at[pl.ds(at, piece.shape[0])], sem.at[i]))
        at += piece.shape[0]
    for c in copies:
        c.start()
    for c in copies:
        c.wait()
    n_rows = 32 * PAY
    each = pbuf.reshape(32, PAY, D)
    r, c = iota((PAY, n_rows), 0), iota((PAY, n_rows), 1)
    place = c - PAY * ((c * 43691) >> 22)
    tot = nn((place == r).astype(BF16), pbuf[...])
    for row, first in [(V_BQ, R_DQ), (V_BV, R_DATT), (V_BO, R_DO), (V_B2, R_DF)] + [
        (V_B1 + j, R_DA + 2 * j) for j in range(4)
    ]:
        vec_out[row : row + 1, :] = tot[first : first + 1, :] + tot[first + 1 : first + 2, :]
    vec_out[V_G1 : V_C1 + 1, :] = tot[R_VEC + 12 : R_VEC + 14, :]
    vec_out[V_G2 : V_C2 + 1, :] = tot[R_VEC + 14 : R_VEC + 16, :]
    vec_out[12:24, :] = tot[R_VEC : R_VEC + 12, :]

    def pick_rows(*firsts):
        r, c = iota((64, n_rows), 0), iota((64, n_rows), 1)
        base = PAY * (r >> 1) + (r & 1)
        select = jnp.concatenate([(c == base + first).astype(BF16) for first in firsts], 0)
        got = nn(select, pbuf[...]).astype(BF16)
        return [got[64 * i : 64 * (i + 1), :] for i in range(len(firsts))]

    def chosen(count, offset, source):
        one_hot = (iota((count, D), 1) == iota((count, D), 0) + offset).astype(BF16)
        return nt(one_hot, source).astype(BF16)

    def put(gi, n, p, value):
        m = GRAN // n
        for j in range(6):
            out[pl.ds(6 * (GRAN * gi + p) + j, m, stride=6 * n), :] = value[:, 128 * j : 128 * (j + 1)]

    @pl.when(info[0] < 8)
    def _():
        off = GRAN * info[0]
        ucls, dq, q, datt = pick_rows(R_U, R_DQ, R_Q, R_DATT)
        parts = [nn(chosen(GRAN, off, ucls), dq)]
        r, c = iota((D, 64), 0), iota((D, 64), 1)
        inside = r - 24 * (c >> 1)
        expand = ((inside >= 0) & (inside < 24) & ((r & 1) == (c & 1))).astype(BF16)
        r = iota((D, D), 0)
        mine = (r - 24 * ((r * 2731) >> 16)) >> 1 == iota((D, D), 1) >> 6
        for right, lo, skip in ((q, 32, 0), (datt, 48, 8)):
            qbuf[...] = jnp.where(mine, nn(expand, right), 0.0).astype(BF16)

            def compact(i, carry, lo=lo, skip=skip):
                rows = each[pl.ds(8 * i, 8), lo : lo + 32, :].astype(F32)
                abuf[pl.ds(pl.multiple_of(192 * i, 192), 192), :] = (
                    rows[:, skip : skip + 24, :].reshape(192, D).astype(BF16)
                )
                return carry

            lax.fori_loop(0, 4, compact, 0)
            parts.append(nn(chosen(GRAN, off, abuf[...]), qbuf[...]))
        for gi in range(3):
            for p in range(3):
                put(gi, 3, p, parts[p][32 * gi : 32 * (gi + 1), :])

    for gi in range(3):
        g = 3 * info[0] + gi

        @pl.when((g >= 24) & (g < 32))
        def _(gi=gi, g=g):
            left, right = pick_rows(R_ATT, R_DO)
            put(gi, 1, 0, nn(chosen(GRAN, GRAN * (g - 24), left), right))

        @pl.when((g >= 32) & (g < 64))
        def _(gi=gi, g=g):
            left, *rights = pick_rows(R_H, *[R_DA + 2 * p for p in range(4)])
            left = chosen(32, 24 * (g - 32), left)
            for p in range(4):
                put(gi, 4, p, nn(left, rights[p])[0:24, :])

        @pl.when(g >= 64)
        def _(gi=gi, g=g):
            left, right = pick_rows(R_E + 2 * ((g - 64) >> 3), R_DF)
            put(gi, 1, 0, nn(chosen(GRAN, GRAN * ((g - 64) & 7), left), right))


def join_grads(info, g0, a, b, gv, out, square, buf):
    g = g0[...]
    out[pl.ds(0, 1728, stride=2), :] = g
    buf[...] = a[...].astype(F32) + b[...].astype(F32)
    total = buf[...]
    sq = jnp.sum((g * g).reshape(216, 8, 128), axis=0)
    for j in range(6):
        v = total[:, 128 * j : 128 * (j + 1)]
        sq = sq + jnp.sum((v * v).reshape(36, 8, 128), axis=0)
    whole = jnp.sum(colsum(sq), axis=1, keepdims=True)
    whole = whole + jnp.sum(colsum(gv[...] * gv[...]), axis=1, keepdims=True)
    square[...] = jnp.broadcast_to(whole, (8, 128))
    for gi in range(3):

        def emit(n, gi=gi):
            m = GRAN // n
            for p in range(n):
                for j in range(6):
                    out[pl.ds(12 * (GRAN * gi + p) + 2 * j + 1, m, stride=12 * n), :] = buf[
                        GRAN * gi + m * p : GRAN * gi + m * (p + 1), 128 * j : 128 * (j + 1)
                    ]

        by_kind(3 * info[0] + gi, emit)


def adamw_kernel(sq, w, m, v, g, vw, vm, vv, vg, w_new, m_new, v_new, vw_new, vm_new, vv_new, norm_out):
    norm = jnp.sqrt(sq[...])
    norm_out[0, 0] = norm[0, 0]
    coef = jnp.minimum(1.0, math.sqrt(2 * (PL + QL)) / (norm[0:1, 0:1] + 1e-06))
    w_new[...], m_new[...], v_new[...] = adamw_update(w[...], m[...], v[...], g[...] * coef, 0.1, weight_decay)
    vw_new[...], vm_new[...], vv_new[...] = adamw_update(vw[...], vm[...], vv[...], vg[...] * coef, 0.5, 0.0)


def adamw_update(weight, moment_one, moment_two, gradient, step_rate, decay_rate):
    first_new = beta_one * moment_one + (1.0 - beta_one) * gradient
    second_new = beta_two * moment_two + (1.0 - beta_two) * gradient * gradient
    first_hat = first_new / (1.0 - beta_one**STEP)
    second_hat = second_new / (1.0 - beta_two**STEP)
    weight_new = weight - step_rate * (first_hat / (jnp.sqrt(second_hat) + adam_epsilon) + decay_rate * weight)
    return (weight_new, first_new, second_new)


def order_kernel(info, a3, a2, mine, came, over_x, over_y, last_x, last_y, o1, o2, o3, o0, acc):
    acc[3], acc[2] = a3[...], a2[...]
    total_kernel(mine, came, over_x, over_y, last_x, last_y, acc.at[1], acc.at[0])
    for k, out in enumerate((o1, o2, o3, o0)):
        out[...] = acc[(info[1] + 3 - k) & 3]


SMEM = pl.BlockSpec(memory_space=pltpu.SMEM)
VMEM = pl.BlockSpec(memory_space=pltpu.VMEM)
ANY = pl.BlockSpec(memory_space=pl.ANY)


def struct(*shape, dtype=F32):
    return jax.ShapeDtypeStruct(shape, dtype)


def call(kernel, name, ins, in_specs, outs, out_specs, scratch=(), flops=0, moved=0):
    return pl.pallas_call(
        kernel,
        out_shape=outs,
        in_specs=in_specs,
        out_specs=out_specs,
        scratch_shapes=list(scratch),
        name=name,
        compiler_params=pltpu.CompilerParams(vmem_limit_bytes=VMEM_BYTES),
        cost_estimate=pl.CostEstimate(flops=flops, bytes_accessed=moved, transcendentals=0),
    )(*ins)


def flat_view(a):
    return a.reshape(2, -1, 128).transpose(1, 0, 2).reshape(-1, 128)


def flat_back(a):
    return a.reshape(-1, 2, 128).transpose(1, 0, 2).reshape(2, -1)


def body(tokens, cotangent, lengths, mats, mats_m, mats_v, vecs, vecs_m, vecs_v):
    dp, pair = lax.axis_index("dp"), lax.axis_index("pair")
    device = 2 * dp + pair
    z = dp >> 2
    info = jnp.stack(
        [device, z, (dp >> 1) & 1, dp & 1, pair, lengths[0, 0, 0], jnp.int32(0), jnp.int32(0)]
    ).astype(jnp.int32)
    u = tokens[0]
    cot = cotangent[0]
    flat = flat_view(mats)
    own = call(pack_kernel, "pack", (info, flat, vecs), [SMEM, VMEM, VMEM], struct(SEND, D, dtype=BF16), VMEM)
    pieces0, pieces1 = gather_blocks(own)
    row = struct(16, D)
    row16 = struct(16, D, dtype=BF16)
    saved_shapes = (
        row, struct(16, 128), row, struct(16, 128), struct(4, 16, D), struct(4, 16, D, dtype=BF16),
        row16, row16, row16, row16, struct(32, D, dtype=BF16), struct(32, D, dtype=BF16), struct(32, TOK),
    )
    weights = [
        pltpu.VMEM((16, D), F32),
        pltpu.VMEM((32, 16, D), BF16),
        pltpu.VMEM((GRANS * GRAN, D), BF16),
        pltpu.VMEM((4, D, D), BF16),
    ]
    y_cls, *saved = call(
        first_forward,
        "first_forward",
        (info, u, *pieces0),
        [SMEM, VMEM] + [ANY] * 32,
        (row, *saved_shapes),
        (VMEM,) * 14,
        weights + [pltpu.SemaphoreType.DMA((64,))],
        flops=2 * 32 * PL,
        moved=2 * PL,
    )
    part = struct(HALF, D, dtype=BF16)
    mid16 = pltpu.VMEM((TOK, D), BF16)
    mid = pltpu.VMEM((TOK, D), F32)
    low = struct(TOK, D, dtype=BF16)
    head_out, dr, vg1, zb, qs, ks, vs, att, pm, w1_grad, theirs_a1, theirs_a2, mine_a1, mine_a2 = call(
        second_block,
        "second_block",
        (info, u, cot, y_cls, *pieces1, *pieces0[3::4]),
        [SMEM, VMEM, VMEM, VMEM] + [ANY] * 40,
        (low, struct(TOK, D), row, low, low, low, low, low, struct(HEADS, TOK, TOK), struct(1536, D, dtype=BF16)) + (part,) * 4,
        (VMEM,) * 8 + (ANY,) * 6,
        weights
        + [
            pltpu.VMEM((GRANS * GRAN, D), BF16),
            mid,
            pltpu.VMEM((HEADS, TOK, TOK), F32),
            mid, mid16,
            pltpu.VMEM((D, TOK), BF16),
            pltpu.VMEM((4, TOK, D), F32),
            pltpu.VMEM((4, TOK, D), BF16),
            pltpu.VMEM((4, TOK, D), BF16),
            mid, mid,
            pltpu.VMEM((8, GRAN, D), F32),
            mid16,
            pltpu.SemaphoreType.DMA((64,)),
            pltpu.SemaphoreType.DMA((30,)),
        ],
        flops=4 * TOK * PL,
        moved=4 * PL,
    )

    def first_part(mine, came):
        return [add16(mine[lo:hi], came[lo:hi]) for lo, hi in ((SX, SY), (SY, QX))]

    def last_part(mine, came, over_x, over_y):
        return [
            (mine[lo : lo + 288].astype(F32) + came[lo : lo + 288].astype(F32) + over[:288].astype(F32)).astype(BF16)
            for lo, over in ((QX - HALF, over_y), (QY - HALF, over_x))
        ]

    own_rows, half = pl.BlockSpec((576, D), lambda i: (1, 0)), pl.BlockSpec((288, D), lambda i: (0, 0))
    second = pl.BlockSpec((288, D), lambda i: (1, 0))

    def plane_total(mine, came, over_x, over_y, last_x, last_y):
        return pl.pallas_call(
            total_kernel,
            grid=(1,),
            in_specs=[own_rows, own_rows, second, second, half, half],
            out_specs=[half, half],
            out_shape=[struct(288, D, dtype=BF16)] * 2,
            name="total",
        )(mine, came, over_x, over_y, last_x, last_y)

    cls = gather_step(y_cls[0:2].astype(BF16), 0, device)()
    theirs_a1, theirs_a2, cls = fence([theirs_a1, theirs_a2, cls])
    came_a1, came_a2 = core_flip(theirs_a1), core_flip(theirs_a2)
    cls = gather_step(cls, 1, device)()
    sx, sy, cls, dr = fence([*first_part(mine_a1, came_a1), cls, dr])
    over_xa, over_ya = x_flip(sx), y_flip(sy)
    dz, vg1, theirs_b1, theirs_b2, mine_b1, mine_b2 = call(
        second_attention,
        "second_attention",
        (info, dr, vg1, zb, qs, ks, vs, att, *pieces1, pm, w1_grad),
        [SMEM] + [VMEM] * 7 + [ANY] * 34,
        (struct(TOK, D), row) + (part,) * 4,
        (VMEM, VMEM) + (ANY,) * 4,
        [
            pltpu.VMEM((GRANS * GRAN // 2, D), BF16),
            pltpu.VMEM((GRANS * GRAN // 2, D), BF16),
            pltpu.VMEM((HEADS, TOK, TOK), F32),
            mid16, mid16, mid16, mid16,
            pltpu.SemaphoreType.DMA((34,)),
        ],
        flops=2 * TOK * PL,
        moved=2 * PL,
    )
    qx_a, qy_a, theirs_b1, theirs_b2, cls = fence(
        [*last_part(mine_a2, came_a2, over_xa, over_ya), theirs_b1, theirs_b2, cls]
    )
    last_xa, last_ya = x_flip(qx_a), y_flip(qy_a)
    came_b1 = core_flip(theirs_b1)
    every_cls = gather_step(cls, 2, device)()
    sx, sy, dz, theirs_b2 = fence([*first_part(mine_b1, came_b1), dz, theirs_b2])
    over_xb, over_yb = x_flip(sx), y_flip(sy)
    came_b2 = core_flip(theirs_b2)
    token_grad, payload, loss = call(
        first_backward,
        "first_backward",
        (info, u, every_cls, dz, vg1, *saved, *pieces0),
        [SMEM] + [VMEM] * 17 + [ANY] * 32,
        (struct(TOK, D), struct(PAY, D, dtype=BF16), struct(1, 1)),
        (VMEM, VMEM, SMEM),
        weights
        + [
            pltpu.VMEM((16, D), F32),
            pltpu.VMEM((64, D), F32),
            pltpu.VMEM((PAY, D), F32),
            pltpu.SemaphoreType.DMA((64,)),
        ],
        flops=2 * 32 * PL,
        moved=2 * PL,
    )
    qx_b, qy_b, pay, last_xa, last_ya = fence(
        [*last_part(mine_b2, came_b2, over_xb, over_yb), payload, last_xa, last_ya]
    )
    last_xb, last_yb = x_flip(qx_b), y_flip(qy_b)
    a3, a2 = plane_total(mine_a2, came_a2, over_xa, over_ya, last_xa, last_ya)
    slots = jnp.concatenate([pay, z_turn(pay, 1), z_turn(pay, 3), z_turn(pay, 2)], 0)
    in_turn = pl.pallas_call(
        order_kernel,
        grid=(1,),
        in_specs=[SMEM, half, half, own_rows, own_rows, second, second, half, half],
        out_specs=[half] * 4,
        out_shape=[struct(288, D, dtype=BF16)] * 4,
        scratch_shapes=[pltpu.VMEM((4, 288, D), BF16)],
        name="order",
    )(info, a3, a2, mine_b2, came_b2, over_xb, over_yb, last_xb, last_yb)
    moving = z_up(in_turn[0])
    over_x, over_y = x_flip(slots), y_flip(slots)
    rows = [slots, over_x, over_y]
    moving = z_up(add16(in_turn[1], moving))
    half = rows[0].shape[0] // 2
    rows += [y_flip(rows[1][:half]), x_flip(rows[2][half:])]
    rows += [core_flip(v) for v in rows]
    moving = z_up(add16(in_turn[2], moving))
    flat0, vec_sum = call(
        owner_grad,
        "owner_grad",
        (info, *rows),
        [SMEM] + [ANY] * 10,
        (struct(1728, 128), struct(24, D)),
        (VMEM, VMEM),
        [
            pltpu.VMEM((32 * PAY, D), BF16),
            pltpu.VMEM((D, D), BF16),
            pltpu.VMEM((D, D), BF16),
            pltpu.SemaphoreType.DMA((10,)),
        ],
        flops=2 * 768 * 768 * 768,
        moved=2 * 32 * PAY * D,
    )
    grad_vecs = lax.dynamic_slice(vec_sum.reshape(2, QL), (0, device * vecs.shape[1]), vecs.shape)
    grads, square = call(
        join_grads,
        "join_grads",
        (info, flat0, in_turn[3], moving, grad_vecs),
        [SMEM] + [VMEM] * 4,
        (struct(3456, 128), struct(8, 128)),
        (VMEM, VMEM),
        [pltpu.VMEM((288, D), F32)],
    )
    block = pl.BlockSpec((864, 128), lambda i: (i, 0))
    small = pl.BlockSpec(vecs.shape, lambda i: (0, 0))
    tile = pl.BlockSpec((8, 128), lambda i: (0, 0))
    *new, new_vecs, new_vecs_m, new_vecs_v, norm = pl.pallas_call(
        adamw_kernel,
        grid=(4,),
        in_specs=[tile] + [block] * 4 + [small] * 4,
        out_specs=(block,) * 3 + (small,) * 3 + (SMEM,),
        out_shape=(struct(3456, 128),) * 3 + (struct(*vecs.shape),) * 3 + (struct(1, 1),),
        name="adamw",
    )(sum_quick(square), flat, flat_view(mats_m), flat_view(mats_v), grads, vecs, vecs_m, vecs_v, grad_vecs)
    new_mats, new_mats_m, new_mats_v = [flat_back(a) for a in new]
    return (
        head_out[None],
        token_grad[None],
        loss.reshape(()),
        norm.reshape(()),
        new_mats,
        new_mats_m,
        new_mats_v,
        new_vecs,
        new_vecs_m,
        new_vecs_v,
    )


def matmul(left_side, right_side):
    return jnp.dot(left_side, right_side, preferred_element_type=jnp.float32)


def inner_rows(left_side, right_side):
    return lax.dot_general(
        left_side, right_side, (((0,), (0,)), ((), ())), preferred_element_type=jnp.float32
    )


def outer_cols(left_side, right_side):
    return lax.dot_general(
        left_side, right_side, (((1,), (1,)), ((), ())), preferred_element_type=jnp.float32
    )


def exact_dot(left_side, right_side):
    return jnp.dot(
        left_side, right_side, precision=lax.Precision.HIGHEST, preferred_element_type=jnp.float32
    )


def layer_norm(resid, gain, shift):
    centred = resid - jnp.mean(resid, axis=-1, keepdims=True)
    spread = jnp.mean(centred * centred, axis=-1, keepdims=True)
    return centred * lax.rsqrt(spread + norm_epsilon) * gain + shift


def gelu_exact(before):
    return jax.nn.gelu(before, approximate=False)


def unpack(mat_row, vec_row):
    edge_one = 3 * D * D
    edge_two = 4 * D * D
    edge_three = edge_two + D * FF
    input_weight = mat_row[:edge_one].reshape(D, 3 * D)
    output_weight = mat_row[edge_one:edge_two].reshape(D, D)
    expand_weight = mat_row[edge_two:edge_three].reshape(D, FF)
    shrink_weight = mat_row[edge_three:].reshape(FF, D)
    vector = vec_row.astype(jnp.float32)
    pieces = []
    cursor = 0
    for piece_len in (D, D, D, D, D, FF, D, D, D):
        pieces.append(vector[cursor : cursor + piece_len])
        cursor = cursor + piece_len
    return (input_weight, output_weight, expand_weight, shrink_weight) + tuple(pieces)


def head_scores(queries, key_rows, same_span):
    row_count = queries.shape[0]
    query_heads = queries.reshape(row_count, HEADS, HEAD_DIM)
    key_heads = key_rows.reshape(row_count, HEADS, HEAD_DIM)
    scores = jnp.einsum(
        "thd,shd->hts", query_heads, key_heads, preferred_element_type=jnp.float32
    ) * HEAD_DIM ** (-0.5)
    return jnp.where(same_span[None, :, :], scores, masked_score)


def layer_forward(params, inputs, same_span):
    (
        input_weight,
        output_weight,
        expand_weight,
        shrink_weight,
        query_bias,
        value_bias,
        output_bias,
        first_gain,
        first_shift,
        expand_bias,
        shrink_bias,
        second_gain,
        second_shift,
    ) = params
    row_count = inputs.shape[0]
    low_input = inputs.astype(jnp.bfloat16)
    joint = matmul(low_input, input_weight)
    queries = (joint[:, :D] + query_bias).astype(jnp.bfloat16)
    key_rows = joint[:, D : 2 * D].astype(jnp.bfloat16)
    values = (joint[:, 2 * D :] + value_bias).astype(jnp.bfloat16)
    scores = head_scores(queries, key_rows, same_span)
    row_max = jnp.max(scores, axis=-1, keepdims=True)
    raised = jnp.exp(scores - row_max)
    summed = jnp.sum(raised, axis=-1, keepdims=True)
    portions = raised / summed
    logsum = row_max + jnp.log(summed)
    value_heads = values.reshape(row_count, HEADS, HEAD_DIM)
    attended = jnp.einsum(
        "hts,shd->thd",
        portions.astype(jnp.bfloat16),
        value_heads,
        preferred_element_type=jnp.float32,
    )
    attended = attended.reshape(row_count, D).astype(jnp.bfloat16)
    resid_one = inputs + (matmul(attended, output_weight) + output_bias)
    hidden = layer_norm(resid_one, first_gain, first_shift)
    low_hidden = hidden.astype(jnp.bfloat16)
    before = matmul(low_hidden, expand_weight) + expand_bias
    activated = gelu_exact(before).astype(jnp.bfloat16)
    resid_two = hidden + (matmul(activated, shrink_weight) + shrink_bias)
    output = layer_norm(resid_two, second_gain, second_shift)
    kept = (
        low_input,
        queries,
        key_rows,
        values,
        logsum,
        attended,
        resid_one,
        low_hidden,
        before,
        activated,
        resid_two,
    )
    return (output, kept)


def layer_backward(params, kept, grad_out, same_span):
    (
        input_weight,
        output_weight,
        expand_weight,
        shrink_weight,
        query_bias,
        value_bias,
        output_bias,
        first_gain,
        first_shift,
        expand_bias,
        shrink_bias,
        second_gain,
        second_shift,
    ) = params
    (
        low_input,
        queries,
        key_rows,
        values,
        logsum,
        attended,
        resid_one,
        low_hidden,
        before,
        activated,
        resid_two,
    ) = kept
    row_count = low_input.shape[0]
    _, norm_pull_two = jax.vjp(layer_norm, resid_two, second_gain, second_shift)
    d_resid_two, d_second_gain, d_second_shift = norm_pull_two(grad_out)
    d_feed = d_resid_two.astype(jnp.bfloat16)
    d_shrink = inner_rows(activated, d_feed)
    d_shrink_bias = jnp.sum(d_feed.astype(jnp.float32), axis=0)
    _, gelu_pull = jax.vjp(gelu_exact, before)
    d_before = gelu_pull(outer_cols(d_feed, shrink_weight))[0].astype(jnp.bfloat16)
    d_expand = inner_rows(low_hidden, d_before)
    d_expand_bias = jnp.sum(d_before.astype(jnp.float32), axis=0)
    d_hidden = d_resid_two + outer_cols(d_before, expand_weight)
    _, norm_pull_one = jax.vjp(layer_norm, resid_one, first_gain, first_shift)
    d_resid_one, d_first_gain, d_first_shift = norm_pull_one(d_hidden)
    d_branch = d_resid_one.astype(jnp.bfloat16)
    d_output = inner_rows(attended, d_branch)
    d_output_bias = jnp.sum(d_branch.astype(jnp.float32), axis=0)
    d_attended = outer_cols(d_branch, output_weight).astype(jnp.bfloat16)
    portions = jnp.exp(head_scores(queries, key_rows, same_span) - logsum)
    query_heads = queries.reshape(row_count, HEADS, HEAD_DIM)
    key_heads = key_rows.reshape(row_count, HEADS, HEAD_DIM)
    value_heads = values.reshape(row_count, HEADS, HEAD_DIM)
    d_att_heads = d_attended.reshape(row_count, HEADS, HEAD_DIM)
    d_portions = jnp.einsum(
        "thd,shd->hts", d_att_heads, value_heads, preferred_element_type=jnp.float32
    )
    d_values = jnp.einsum(
        "hts,thd->shd",
        portions.astype(jnp.bfloat16),
        d_att_heads,
        preferred_element_type=jnp.float32,
    )
    d_values = d_values.reshape(row_count, D).astype(jnp.bfloat16)
    d_scores = portions * (d_portions - jnp.sum(d_portions * portions, axis=-1, keepdims=True))
    d_scores = d_scores.astype(jnp.bfloat16)
    score_scale = HEAD_DIM ** (-0.5)
    d_queries = (
        jnp.einsum("hts,shd->thd", d_scores, key_heads, preferred_element_type=jnp.float32)
        * score_scale
    )
    d_queries = d_queries.reshape(row_count, D).astype(jnp.bfloat16)
    d_keys = (
        jnp.einsum("hts,thd->shd", d_scores, query_heads, preferred_element_type=jnp.float32)
        * score_scale
    )
    d_keys = d_keys.reshape(row_count, D).astype(jnp.bfloat16)
    d_joint = jnp.concatenate([d_queries, d_keys, d_values], axis=1)
    d_input_weight = inner_rows(low_input, d_joint)
    d_query_bias = jnp.sum(d_queries.astype(jnp.float32), axis=0)
    d_value_bias = jnp.sum(d_values.astype(jnp.float32), axis=0)
    d_inputs = d_resid_one + outer_cols(d_joint, input_weight)
    mat_grad = jnp.concatenate(
        [
            d_input_weight.reshape(-1),
            d_output.reshape(-1),
            d_expand.reshape(-1),
            d_shrink.reshape(-1),
        ]
    )
    vec_grad = jnp.concatenate(
        [
            d_query_bias,
            d_value_bias,
            d_output_bias,
            d_first_gain,
            d_first_shift,
            d_expand_bias,
            d_shrink_bias,
            d_second_gain,
            d_second_shift,
        ]
    )
    return (d_inputs, mat_grad, vec_grad)


def contrast_rows(anchors, key_table, anchor_index, span_count, score_scale):
    key_count = key_table.shape[0]
    key_index = jnp.arange(key_count, dtype=jnp.int32)
    scores = outer_cols(anchors, key_table) * score_scale
    scores = jnp.where(anchor_index[:, None] == key_index[None, :], masked_score, scores)
    partner = (
        jnp.bitwise_xor(anchor_index // span_count, 1) * span_count + anchor_index % span_count
    )
    row_max = jnp.max(scores, axis=-1, keepdims=True)
    raised = jnp.exp(scores - row_max)
    summed = jnp.sum(raised, axis=-1, keepdims=True)
    logsum = row_max[:, 0] + jnp.log(summed[:, 0])
    target = key_index[None, :] == partner[:, None]
    positive = jnp.sum(jnp.where(target, scores, 0.0), axis=1)
    grads_low = (raised / summed - target.astype(jnp.float32)).astype(jnp.bfloat16)
    return (grads_low, logsum - positive)


def general_body(tokens, cotangent, lengths, mats, mats_m, mats_v, vecs, vecs_m, vecs_v):
    full_mats, full_vecs = (
        lax.all_gather(mats.astype(jnp.bfloat16), ("dp", "pair"), axis=1, tiled=True),
        lax.all_gather(vecs.astype(jnp.bfloat16), ("dp", "pair"), axis=1, tiled=True),
    )
    layer_one = unpack(full_mats[0], full_vecs[0])
    layer_two = unpack(full_mats[1], full_vecs[1])
    inputs = tokens[0].astype(jnp.float32)
    row_count = inputs.shape[0]
    span_lengths = lengths[0, 0]
    span_count = span_lengths.shape[0]
    positions = jnp.arange(row_count, dtype=jnp.int32)
    order = jnp.arange(span_count)
    starts = jnp.sum(jnp.where(order[None, :] < order[:, None], span_lengths[None, :], 0), axis=1)
    span_of = jnp.sum((positions[:, None] >= starts[None, :]).astype(jnp.int32), axis=1)
    same_span = span_of[:, None] == span_of[None, :]
    heads_mark = positions[None, :] == starts[:, None]
    is_cls = jnp.any(heads_mark, axis=0)[:, None]
    picker = heads_mark.astype(jnp.float32)
    doc_groups = lax.axis_size("dp")
    early_out, kept_one = layer_forward(layer_one, inputs, same_span)
    cls_rows = exact_dot(picker, early_out)
    mixture = jnp.where(is_cls, early_out, inputs)
    late_out, kept_two = layer_forward(layer_two, mixture, same_span)
    sent_cls = cls_rows.astype(jnp.bfloat16)
    every_cls = lax.all_gather(sent_cls, ("dp", "pair"), axis=0, tiled=True)
    key_count = every_cls.shape[0]
    score_scale = 2.0 / math.sqrt(D)
    offset = lax.axis_index(("dp", "pair")) * span_count
    own_index = offset + jnp.arange(span_count, dtype=jnp.int32)
    grads_low, loss_terms = contrast_rows(sent_cls, every_cls, own_index, span_count, score_scale)
    anchor_part = matmul(grads_low, every_cls) * score_scale
    key_part = lax.psum_scatter(
        inner_rows(grads_low, sent_cls) * score_scale,
        ("dp", "pair"),
        scatter_dimension=0,
        tiled=True,
    )
    cls_grad = anchor_part + key_part
    grad_late = cotangent[0].astype(jnp.float32)
    d_mixture, late_mats, late_vecs = layer_backward(layer_two, kept_two, grad_late, same_span)
    grad_early = jnp.where(is_cls, d_mixture, 0.0) + exact_dot(picker.T, cls_grad)
    d_inputs, early_mats, early_vecs = layer_backward(layer_one, kept_one, grad_early, same_span)
    token_grad = d_inputs + jnp.where(is_cls, 0.0, d_mixture)
    all_pieces = (
        lax.all_to_all(
            early_mats.reshape(doc_groups, -1).astype(jnp.bfloat16),
            "dp",
            split_axis=0,
            concat_axis=0,
            tiled=True,
        ).astype(jnp.float32),
        lax.all_to_all(
            late_mats.reshape(doc_groups, -1).astype(jnp.bfloat16),
            "dp",
            split_axis=0,
            concat_axis=0,
            tiled=True,
        ).astype(jnp.float32),
        lax.all_to_all(
            early_vecs.reshape(doc_groups, -1).astype(jnp.bfloat16),
            "dp",
            split_axis=0,
            concat_axis=0,
            tiled=True,
        ).astype(jnp.float32),
        lax.all_to_all(
            late_vecs.reshape(doc_groups, -1).astype(jnp.bfloat16),
            "dp",
            split_axis=0,
            concat_axis=0,
            tiled=True,
        ).astype(jnp.float32),
    )
    early_mats_part, late_mats_part, early_vecs_part, late_vecs_part = (
        lax.psum_scatter(
            jnp.sum(all_pieces[0], axis=0).astype(jnp.bfloat16),
            "pair",
            scatter_dimension=0,
            tiled=True,
        ).astype(jnp.float32),
        lax.psum_scatter(
            jnp.sum(all_pieces[1], axis=0).astype(jnp.bfloat16),
            "pair",
            scatter_dimension=0,
            tiled=True,
        ).astype(jnp.float32),
        lax.psum_scatter(
            jnp.sum(all_pieces[2], axis=0).astype(jnp.bfloat16),
            "pair",
            scatter_dimension=0,
            tiled=True,
        ).astype(jnp.float32),
        lax.psum_scatter(
            jnp.sum(all_pieces[3], axis=0).astype(jnp.bfloat16),
            "pair",
            scatter_dimension=0,
            tiled=True,
        ).astype(jnp.float32),
    )
    grad_mats = jnp.stack([early_mats_part, late_mats_part])
    grad_vecs = jnp.stack([early_vecs_part, late_vecs_part])
    square_sum = jnp.sum(grad_mats * grad_mats) + jnp.sum(grad_vecs * grad_vecs)
    total_sq, loss_sum = lax.psum((square_sum, jnp.sum(loss_terms)), ("dp", "pair"))
    grad_norm = jnp.sqrt(total_sq)
    clip_factor = jnp.minimum(1.0, math.sqrt(2 * (PL + QL)) / (grad_norm + 1e-06))
    new_mats, new_mats_m, new_mats_v = adamw_update(
        mats, mats_m, mats_v, grad_mats * clip_factor, 0.1, weight_decay
    )
    new_vecs, new_vecs_m, new_vecs_v = adamw_update(
        vecs, vecs_m, vecs_v, grad_vecs * clip_factor, 0.5, 0.0
    )
    contrastive = loss_sum / key_count
    return (
        late_out.astype(jnp.bfloat16)[None],
        token_grad[None],
        contrastive,
        grad_norm,
        new_mats,
        new_mats_m,
        new_mats_v,
        new_vecs,
        new_vecs_m,
        new_vecs_v,
    )


def solution(mesh):
    flat = P(None, ("dp", "pair"))
    rows = P("pair", "dp", None)
    here = dict(mesh.shape) == {"dp": 16, "pair": 2}
    return jax.shard_map(
        body if here else general_body,
        mesh=mesh,
        in_specs=(rows, rows, rows) + (flat,) * 6,
        out_specs=(rows, rows, P(), P()) + (flat,) * 6,
        check_vma=False,
    )
```

profile of v0, /device:TPU:0, one launch (start us, length us, event | category | flops | bytes accessed | tf_op | source)
XLA Modules:
  0.0 350.3 jit_solution(1793993798092439534)
XLA Ops:
  11.1 16.9 %collective-permute-done.refs_1_ = bf16[592,768]{1,0:T(8,128)(2,1)S(1)} collective-permute-done((bf16[592,768]{1,0:T(8,128)(2,1)}, bf16[592,768]{1,0:T(8,128)(2,1)S(1)}, u32[]{:S(2)}, u32[]{:S(2)}) %collective-permute-start) | collective-permute-done | bytes 909344 | tf_op jit(solution)/shard_map/ppermute | solution.py:98
  29.4 3.1 collective-permute-done.2.refs_4_
  36.9 25.7 %collective-permute-done.4.refs_3_ = bf16[288,768]{1,0:T(8,128)(2,1)} collective-permute-done((bf16[288,768]{1,0:T(8,128)(2,1)S(1)}, bf16[288,768]{1,0:T(8,128)(2,1)}, u32[]{:S(2)}, u32[]{:S(2)}) %collective-permute-start.4) | collective-permute-done | bytes 442400 | tf_op jit(solution)/shard_map/ppermute | solution.py:98
  68.4 24.0 %collective-permute-done.9.refs_7_ = bf16[288,768]{1,0:T(8,128)(2,1)} collective-permute-done((bf16[288,768]{1,0:T(8,128)(2,1)S(1)}, bf16[288,768]{1,0:T(8,128)(2,1)}, u32[]{:S(2)}, u32[]{:S(2)}) %collective-permute-start.9) | collective-permute-done | bytes 442400 | tf_op jit(solution)/shard_map/ppermute | solution.py:98
  99.3 27.6 %collective-permute-done.14.refs_11_ = bf16[288,768]{1,0:T(8,128)(2,1)} collective-permute-done((bf16[288,768]{1,0:T(8,128)(2,1)S(1)}, bf16[288,768]{1,0:T(8,128)(2,1)}, u32[]{:S(2)}, u32[]{:S(2)}) %collective-permute-start.14) | collective-permute-done | bytes 442400 | tf_op jit(solution)/shard_map/ppermute | solution.py:98
  133.5 11.1 %collective-permute-done.34.refs_15_ = bf16[288,768]{1,0:T(8,128)(2,1)} collective-permute-done((bf16[288,768]{1,0:T(8,128)(2,1)S(1)}, bf16[288,768]{1,0:T(8,128)(2,1)}, u32[]{:S(2)}, u32[]{:S(2)}) %collective-permute-start.34) | collective-permute-done | bytes 442400 | tf_op jit(solution)/shard_map/ppermute | solution.py:98
  153.5 9.6 %first_forward.1 = (f32[16,768]{1,0:T(8,128)}, f32[16,768]{1,0:T(8,128)}, f32[16,128]{1,0:T(8,128)}, f32[16,768]{1,0:T(8,128)}, f32[16,128]{1,0:T(8,128)}, /*ind...) custom-call(s32[8]{0:T(128)} %stack.23.info, ...), custom_call_target="tpu_custom_call" | custom-call | flops 452984832 | bytes 14155776 | tf_op jit(solution)/shard_map/first_forward/pallas_call | solution.py:804
  166.0 23.5 %second_block.1 = (bf16[256,768]{1,0:T(8,128)(2,1)}, f32[256,768]{1,0:T(8,128)}, f32[16,768]{1,0:T(8,128)}, bf16[256,768]{1,0:T(8,128)(2,1)}, bf16[256,768]{1,0:...) custom-call(s32[8]{0:T(128)} %stack.23.info, ...), custom_call_target="tpu_custom_call" | custom-call | flops 7247757312 | bytes 28311552 | tf_op jit(solution)/shard_map/second_block/pallas_call | solution.py:804
  198.9 3.1 add_convert_fusion.2
  203.7 14.4 %second_attention.1 = (f32[256,768]{1,0:T(8,128)}, f32[16,768]{1,0:T(8,128)}, bf16[1152,768]{1,0:T(8,128)(2,1)}, bf16[1152,768]{1,0:T(8,128)(2,1)}, bf16[1152,76...) custom-call(s32[8]{0:T(128)} %stack.23.info, f32[256,768]{1,0:T(8,128)} %get-tuple-element.169.dr, ...), custom_call_target="tpu_custom_call" | custom-call | flops 3623878656 | bytes 14155776 | tf_op jit(solution)/shard_map/second_attention/pallas_call | solution.py:804
  218.2 4.1 %collective-permute-done.47.over_y = bf16[576,768]{1,0:T(8,128)(2,1)} collective-permute-done((bf16[576,768]{1,0:T(8,128)(2,1)}, bf16[576,768]{1,0:T(8,128)(2,1)}, u32[]{:S(2)}, u32[]{:S(2)}) %collective-permute-start.47) | collective-permute-done | bytes 884768 | tf_op jit(solution)/shard_map/ppermute | solution.py:98
  225.6 3.7 %collective-permute-done.50 = bf16[1152,768]{1,0:T(8,128)(2,1)S(1)} collective-permute-done((bf16[1152,768]{1,0:T(8,128)(2,1)S(1)}, bf16[1152,768]{1,0:T(8,128)(2,1)S(1)}, u32[]{:S(2)}, u32[]{:S(2)}) %collective-permute-start.50) | collective-permute-done | bytes 1769504 | tf_op jit(solution)/shard_map/ppermute | solution.py:98
  241.3 14.5 %first_backward.1 = (f32[256,768]{1,0:T(8,128)}, bf16[96,768]{1,0:T(8,128)(2,1)}, f32[1,1]{1,0:T(1,128)}) custom-call(s32[8]{0:T(128)} %stack.23.info, bf16[256,768]{1,0:T(8,128)(2,1)} %bitcast.47, bf16[64,768]{1,0:T(8,128)(2,1)} %pad_maximum_fusion.cls_all, f32[256,768]{1,0:T(8,128)} %get-tuple-element.186.dz, f32[16,768]{1,0:T(8,128)} %get-tuple-element.187.vg1, ...), custom_call_target="tpu_custom_call" | custom-call | flops 452984832 | bytes 14155776 | tf_op jit(solution)/shard_map/first_backward/pallas_call | solution.py:804
  255.9 3.0 add_convert_fusion.6
  258.9 4.6 %collective-permute-done.54.last_x = bf16[288,768]{1,0:T(8,128)(2,1)S(1)} collective-permute-done((bf16[288,768]{1,0:T(8,128)(2,1)}, bf16[288,768]{1,0:T(8,128)(2,1)S(1)}, u32[]{:S(2)}, u32[]{:S(2)}) %collective-permute-start.54) | collective-permute-done | bytes 442400 | tf_op jit(solution)/shard_map/ppermute | solution.py:98
  270.3 3.2 total.1
  276.1 4.3 %order.1 = (bf16[288,768]{1,0:T(8,128)(2,1)}, bf16[288,768]{1,0:T(8,128)(2,1)}, bf16[288,768]{1,0:T(8,128)(2,1)}, bf16[288,768]{1,0:T(8,128)(2,1)}) custom-call(s32[8]{0:T(128)} %stack.23.info, bf16[288,768]{1,0:T(8,128)(2,1)} %get-tuple-element.214.a3, bf16[288,768]{1,0:T(8,128)(2,1)} %get-tuple-element.215.a2, bf16[1152,768]{1,0:T(8,128)(2,1)} %get-tuple-element.203.mine, ...), custom_call_target="tpu_custom_call" | custom-call | tf_op jit(solution)/shard_map/order/pallas_call | solution.py:967
  280.4 3.1 collective-permute-start.70
  284.6 8.2 %collective-permute-done.70 = bf16[288,768]{1,0:T(8,128)(2,1)S(1)} collective-permute-done((bf16[288,768]{1,0:T(8,128)(2,1)}, bf16[288,768]{1,0:T(8,128)(2,1)S(1)}, u32[]{:S(2)}, u32[]{:S(2)}) %collective-permute-start.70) | collective-permute-done | bytes 442400 | tf_op jit(solution)/shard_map/ppermute | solution.py:115
  299.3 3.2 collective-permute-done.61.refs_3_
  302.4 3.9 %collective-permute-done.62.refs_4_ = bf16[192,768]{1,0:T(8,128)(2,1)} collective-permute-done((bf16[192,768]{1,0:T(8,128)(2,1)S(1)}, bf16[192,768]{1,0:T(8,128)(2,1)}, u32[]{:S(2)}, u32[]{:S(2)}) %collective-permute-start.62) | collective-permute-done | bytes 294944 | tf_op jit(solution)/shard_map/ppermute | solution.py:98
  310.5 10.1 %owner_grad.1 = (f32[1728,128]{1,0:T(8,128)}, f32[24,768]{1,0:T(8,128)}) custom-call(s32[8]{0:T(128)} %stack.23.info, bf16[384,768]{1,0:T(8,128)(2,1)} %copy-done.37, bf16[384,768]{1,0:T(8,128)(2,1)} %copy-done.35, bf16[384,768]{1,0:T(8,128)(2,1)} %copy-done.36, bf16[192,768]{1,0:T(8,128)(2,1)} %collective-permute-done.61.refs_3_, ...), custom_call_target="tpu_custom_call" | custom-call | flops 905969664 | bytes 4718592 | tf_op jit(solution)/shard_map/owner_grad/pallas_call | solution.py:804
  323.0 3.2 join_grads.1
  343.3 6.5 %adamw.1 = (f32[3456,128]{1,0:T(8,128)}, f32[3456,128]{1,0:T(8,128)}, f32[3456,128]{1,0:T(8,128)}, f32[2,288]{1,0:T(2,128)}, f32[2,288]{1,0:T(2,128)}, /*index=5*/f32[2,288]{1,0:T(2,128)}, f32[1,1]{1,0:T(1,128)}) custom-call(f32[8,128]{1,0:T(8,128)} %add_add_fusion.sq, f32[3456,128]{1,0:T(8,128)} %bitcast.44, f32[3456,128]{1,0:T(8,128)} %bitcast.48, ...), custom_call_target="tpu_custom_call" | custom-call | tf_op jit(solution)/shard_map/adamw/pallas_call | solution.py:1013
  (274 shorter events, 113.9 us)
Async XLA Ops:
  32.6 30.8 %collective-permute-start.5 = (bf16[592,768]{1,0:T(8,128)(2,1)S(1)}, bf16[592,768]{1,0:T(8,128)(2,1)S(1)}, u32[]{:S(2)}, u32[]{:S(2)}) collective-permute-start(bf16[592,768]{1,0:T(8,128)(2,1)S(1)} %collective-permute-done.2.refs_4_), channel_id=1, source_target_pairs={{0,4},{2,6},{4,0},{6,2},{8,12},{10,14},{12,8},{14,10},{16,20},{18,... | collective-permute-start | bytes 2727944 | tf_op jit(solution)/shard_map/ppermute | solution.py:98
  33.1 30.3 %collective-permute-start.6 = (bf16[592,768]{1,0:T(8,128)(2,1)S(1)}, bf16[592,768]{1,0:T(8,128)(2,1)S(1)}, u32[]{:S(2)}, u32[]{:S(2)}) collective-permute-start(bf16[592,768]{1,0:T(8,128)(2,1)S(1)} %collective-permute-done.2.refs_4_), channel_id=1, source_target_pairs={{0,1},{1,0},{2,3},{3,2},{4,5},{5,4},{6,7},{7,6},{8,9},{9,8},{10,11... | collective-permute-start | bytes 2727944 | tf_op jit(solution)/shard_map/ppermute | solution.py:98
  33.6 29.8 %collective-permute-start.7 = (bf16[592,768]{1,0:T(8,128)(2,1)S(1)}, bf16[592,768]{1,0:T(8,128)(2,1)S(1)}, u32[]{:S(2)}, u32[]{:S(2)}) collective-permute-start(bf16[592,768]{1,0:T(8,128)(2,1)S(1)} %collective-permute-done.2.refs_4_), channel_id=1, source_target_pairs={{0,8},{2,10},{4,12},{6,14},{8,16},{10,18},{12,20},{14,22},{16,24},... | collective-permute-start | bytes 2727944 | tf_op jit(solution)/shard_map/ppermute | solution.py:115
  33.6 29.7 %collective-permute-start.3 = (bf16[304,768]{1,0:T(8,128)(2,1)S(1)}, bf16[304,768]{1,0:T(8,128)(2,1)S(1)}, u32[]{:S(2)}, u32[]{:S(2)}) collective-permute-start(bf16[304,768]{1,0:T(8,128)(2,1)S(1)} %slice.98), channel_id=1, source_target_pairs={{0,1},{1,0},{2,3},{3,2},{4,5},{5,4},{6,7},{7,6},{8,9},{9,8},{10,11... | collective-permute-start | bytes 1400840 | tf_op jit(solution)/shard_map/ppermute | solution.py:98
  35.4 27.3 %collective-permute-start.4 = (bf16[288,768]{1,0:T(8,128)(2,1)S(1)}, bf16[288,768]{1,0:T(8,128)(2,1)}, u32[]{:S(2)}, u32[]{:S(2)}) collective-permute-start(bf16[288,768]{1,0:T(8,128)(2,1)S(1)} %slice.99), channel_id=1, source_target_pairs={{0,4},{2,6},{4,0},{6,2},{8,12},{10,14},{12,8},{14,10},{16,20},{18,... | collective-permute-start | bytes 1327112 | tf_op jit(solution)/shard_map/ppermute | solution.py:98
  63.4 30.7 %collective-permute-start.10 = (bf16[592,768]{1,0:T(8,128)(2,1)S(1)}, bf16[592,768]{1,0:T(8,128)(2,1)S(1)}, u32[]{:S(2)}, u32[]{:S(2)}) collective-permute-start(bf16[592,768]{1,0:T(8,128)(2,1)S(1)} %collective-permute-done.7.refs_8_), channel_id=1, source_target_pairs={{0,4},{2,6},{4,0},{6,2},{8,12},{10,14},{12,8},{14,10},{16,20},{18,... | collective-permute-start | bytes 2727944 | tf_op jit(solution)/shard_map/ppermute | solution.py:98
  64.9 29.7 %collective-permute-start.11 = (bf16[592,768]{1,0:T(8,128)(2,1)S(1)}, bf16[592,768]{1,0:T(8,128)(2,1)S(1)}, u32[]{:S(2)}, u32[]{:S(2)}) collective-permute-start(bf16[592,768]{1,0:T(8,128)(2,1)S(1)} %collective-permute-done.7.refs_8_), channel_id=1, source_target_pairs={{0,1},{1,0},{2,3},{3,2},{4,5},{5,4},{6,7},{7,6},{8,9},{9,8},{10,11... | collective-permute-start | bytes 2727944 | tf_op jit(solution)/shard_map/ppermute | solution.py:98
  65.5 27.0 %collective-permute-start.9 = (bf16[288,768]{1,0:T(8,128)(2,1)S(1)}, bf16[288,768]{1,0:T(8,128)(2,1)}, u32[]{:S(2)}, u32[]{:S(2)}) collective-permute-start(bf16[288,768]{1,0:T(8,128)(2,1)S(1)} %slice.101), channel_id=1, source_target_pairs={{0,4},{2,6},{4,0},{6,2},{8,12},{10,14},{12,8},{14,10},{16,20},{18,... | collective-permute-start | bytes 1327112 | tf_op jit(solution)/shard_map/ppermute | solution.py:98
  66.3 27.8 %collective-permute-start.8 = (bf16[304,768]{1,0:T(8,128)(2,1)S(1)}, bf16[304,768]{1,0:T(8,128)(2,1)S(1)}, u32[]{:S(2)}, u32[]{:S(2)}) collective-permute-start(bf16[304,768]{1,0:T(8,128)(2,1)S(1)} %slice.100), channel_id=1, source_target_pairs={{0,1},{1,0},{2,3},{3,2},{4,5},{5,4},{6,7},{7,6},{8,9},{9,8},{10,11... | collective-permute-start | bytes 1400840 | tf_op jit(solution)/shard_map/ppermute | solution.py:98
  67.7 27.1 %collective-permute-start.12 = (bf16[592,768]{1,0:T(8,128)(2,1)S(1)}, bf16[592,768]{1,0:T(8,128)(2,1)S(1)}, u32[]{:S(2)}, u32[]{:S(2)}) collective-permute-start(bf16[592,768]{1,0:T(8,128)(2,1)S(1)} %collective-permute-done.7.refs_8_), channel_id=1, source_target_pairs={{0,8},{2,10},{4,12},{6,14},{8,16},{10,18},{12,20},{14,22},{16,24},... | collective-permute-start | bytes 2727944 | tf_op jit(solution)/shard_map/ppermute | solution.py:115
  94.8 32.6 %collective-permute-start.15 = (bf16[592,768]{1,0:T(8,128)(2,1)S(1)}, bf16[592,768]{1,0:T(8,128)(2,1)S(1)}, u32[]{:S(2)}, u32[]{:S(2)}) collective-permute-start(bf16[592,768]{1,0:T(8,128)(2,1)S(1)} %collective-permute-done.12.refs_12_), channel_id=1, source_target_pairs={{0,4},{2,6},{4,0},{6,2},{8,12},{10,14},{12,8},{14,10},{16,20},{18,... | collective-permute-start | bytes 2727944 | tf_op jit(solution)/shard_map/ppermute | solution.py:98
  95.4 31.5 %collective-permute-start.14 = (bf16[288,768]{1,0:T(8,128)(2,1)S(1)}, bf16[288,768]{1,0:T(8,128)(2,1)}, u32[]{:S(2)}, u32[]{:S(2)}) collective-permute-start(bf16[288,768]{1,0:T(8,128)(2,1)S(1)} %slice.103), channel_id=1, source_target_pairs={{0,4},{2,6},{4,0},{6,2},{8,12},{10,14},{12,8},{14,10},{16,20},{18,... | collective-permute-start | bytes 1327112 | tf_op jit(solution)/shard_map/ppermute | solution.py:98
  97.0 29.9 %collective-permute-start.13 = (bf16[304,768]{1,0:T(8,128)(2,1)S(1)}, bf16[304,768]{1,0:T(8,128)(2,1)S(1)}, u32[]{:S(2)}, u32[]{:S(2)}) collective-permute-start(bf16[304,768]{1,0:T(8,128)(2,1)S(1)} %slice.102), channel_id=1, source_target_pairs={{0,1},{1,0},{2,3},{3,2},{4,5},{5,4},{6,7},{7,6},{8,9},{9,8},{10,11... | collective-permute-start | bytes 1400840 | tf_op jit(solution)/shard_map/ppermute | solution.py:98
  97.9 31.1 %collective-permute-start.16 = (bf16[592,768]{1,0:T(8,128)(2,1)S(1)}, bf16[592,768]{1,0:T(8,128)(2,1)S(1)}, u32[]{:S(2)}, u32[]{:S(2)}) collective-permute-start(bf16[592,768]{1,0:T(8,128)(2,1)S(1)} %collective-permute-done.12.refs_12_), channel_id=1, source_target_pairs={{0,1},{1,0},{2,3},{3,2},{4,5},{5,4},{6,7},{7,6},{8,9},{9,8},{10,11... | collective-permute-start | bytes 2727944 | tf_op jit(solution)/shard_map/ppermute | solution.py:98
  99.2 32.7 %collective-permute-start.23 = (bf16[592,768]{1,0:T(8,128)(2,1)S(1)}, bf16[592,768]{1,0:T(8,128)(2,1)S(1)}, u32[]{:S(2)}, u32[]{:S(2)}) collective-permute-start(bf16[592,768]{1,0:T(8,128)(2,1)S(1)} %collective-permute-done.5.refs_5_), channel_id=1, source_target_pairs={{0,2},{2,0},{4,6},{6,4},{8,10},{10,8},{12,14},{14,12},{16,18},{18,... | collective-permute-start | bytes 2727944 | tf_op jit(solution)/shard_map/ppermute | solution.py:98
  163.9 25.7 %collective-permute-start.39 = (bf16[2,768]{1,0:T(2,128)(2,1)S(1)}, bf16[2,768]{1,0:T(2,128)(2,1)S(1)}, u32[]{:S(2)}, u32[]{:S(2)}) collective-permute-start(bf16[2,768]{1,0:T(2,128)(2,1)S(1)} %slice.165), channel_id=1, source_target_pairs={{0,1},{1,0},{2,3},{3,2},{4,5},{5,4},{6,7},{7,6},{8,9},{9,8},{10,11... | collective-permute-start | bytes 9224 | tf_op jit(solution)/shard_map/ppermute | solution.py:127
  165.4 24.2 %collective-permute-start.40 = (bf16[2,768]{1,0:T(2,128)(2,1)S(1)}, bf16[2,768]{1,0:T(2,128)(2,1)S(1)}, u32[]{:S(2)}, u32[]{:S(2)}) collective-permute-start(bf16[2,768]{1,0:T(2,128)(2,1)S(1)} %slice.165), channel_id=1, source_target_pairs={{0,2},{2,0},{4,6},{6,4},{8,10},{10,8},{12,14},{14,12},{16,18},{18,... | collective-permute-start | bytes 9224 | tf_op jit(solution)/shard_map/ppermute | solution.py:98
  165.5 24.1 %collective-permute-start.41 = (bf16[2,768]{1,0:T(2,128)(2,1)S(1)}, bf16[2,768]{1,0:T(2,128)(2,1)S(1)}, u32[]{:S(2)}, u32[]{:S(2)}) collective-permute-start(bf16[2,768]{1,0:T(2,128)(2,1)S(1)} %slice.165), channel_id=1, source_target_pairs={{0,3},{1,2},{2,1},{3,0},{4,7},{5,6},{6,5},{7,4},{8,11},{9,10},{10,... | collective-permute-start | bytes 9224 | tf_op jit(solution)/shard_map/ppermute | solution.py:127
  190.6 27.6 %collective-permute-start.42 = (bf16[1152,768]{1,0:T(8,128)(2,1)}, bf16[1152,768]{1,0:T(8,128)(2,1)S(1)}, u32[]{:S(2)}, u32[]{:S(2)}) collective-permute-start(bf16[1152,768]{1,0:T(8,128)(2,1)} %get-tuple-element.162), channel_id=1, source_target_pairs={{0,2},{2,0},{4,6},{6,4},{8,10},{10,8},{12,14},{14,12},{16,18},{18,... | collective-permute-start | bytes 5308424 | tf_op jit(solution)/shard_map/ppermute | solution.py:98
  231.0 24.8 %collective-permute-start.51 = (bf16[1152,768]{1,0:T(8,128)(2,1)}, bf16[1152,768]{1,0:T(8,128)(2,1)S(1)}, u32[]{:S(2)}, u32[]{:S(2)}) collective-permute-start(bf16[1152,768]{1,0:T(8,128)(2,1)} %get-tuple-element.204), channel_id=1, source_target_pairs={{0,2},{2,0},{4,6},{6,4},{8,10},{10,8},{12,14},{14,12},{16,18},{18,... | collective-permute-start | bytes 5308424 | tf_op jit(solution)/shard_map/ppermute | solution.py:98
  231.1 24.7 %collective-permute-start.52 = (bf16[576,768]{1,0:T(8,128)(2,1)}, bf16[576,768]{1,0:T(8,128)(2,1)}, u32[]{:S(2)}, u32[]{:S(2)}) collective-permute-start(bf16[576,768]{1,0:T(8,128)(2,1)} %get-tuple-element.205), channel_id=1, source_target_pairs={{0,1},{1,0},{2,3},{3,2},{4,5},{5,4},{6,7},{7,6},{8,9},{9,8},{10,11... | collective-permute-start | bytes 2654216 | tf_op jit(solution)/shard_map/ppermute | solution.py:98
  232.1 23.7 %collective-permute-start.53 = (bf16[576,768]{1,0:T(8,128)(2,1)}, bf16[576,768]{1,0:T(8,128)(2,1)}, u32[]{:S(2)}, u32[]{:S(2)}) collective-permute-start(bf16[576,768]{1,0:T(8,128)(2,1)} %get-tuple-element.206), channel_id=1, source_target_pairs={{0,4},{2,6},{4,0},{6,2},{8,12},{10,14},{12,8},{14,10},{16,20},{18,... | collective-permute-start | bytes 2654216 | tf_op jit(solution)/shard_map/ppermute | solution.py:98
  234.7 28.8 %collective-permute-start.54 = (bf16[288,768]{1,0:T(8,128)(2,1)}, bf16[288,768]{1,0:T(8,128)(2,1)S(1)}, u32[]{:S(2)}, u32[]{:S(2)}) collective-permute-start(bf16[288,768]{1,0:T(8,128)(2,1)} %get-tuple-element.208), channel_id=1, source_target_pairs={{0,4},{2,6},{4,0},{6,2},{8,12},{10,14},{12,8},{14,10},{16,20},{18,... | collective-permute-start | bytes 1327112 | tf_op jit(solution)/shard_map/ppermute | solution.py:98
  238.3 25.1 %collective-permute-start.55 = (bf16[288,768]{1,0:T(8,128)(2,1)}, bf16[288,768]{1,0:T(8,128)(2,1)}, u32[]{:S(2)}, u32[]{:S(2)}) collective-permute-start(bf16[288,768]{1,0:T(8,128)(2,1)} %get-tuple-element.209), channel_id=1, source_target_pairs={{0,1},{1,0},{2,3},{3,2},{4,5},{5,4},{6,7},{7,6},{8,9},{9,8},{10,11... | collective-permute-start | bytes 1327112 | tf_op jit(solution)/shard_map/ppermute | solution.py:98
  (103 other events, 1895.9 us)
where the time goes:
time: 353 us; the launch traced here: 350 us
  waiting for transfers between devices  168 us (48%)
  Pallas kernels  92 us (26%)
  starting transfers between devices  62.3 us (18%)
  other arithmetic  17.3 us (5%)
  local copies, waits for them, and re-layouts  9.15 us (3%)
    ppermute x67, waiting for transfers between devices, flip(): lax.ppermute(v, axis, [(i, i ^ bit) for i in range(lax.axis_size(axis))])  154 us
    pallas_call x7, Pallas kernels, call(): pl.pallas_call(kernel, out_shape=outs, in_specs=in_specs, out_specs=out_s...  78 us
    ppermute x67, starting transfers between devices, flip(): lax.ppermute(v, axis, [(i, i ^ bit) for i in range(lax.axis_size(axis))])  45 us
    ppermute x6, waiting for transfers between devices, z_up(): return lax.ppermute(v, 'dp', [(i, (i + 4) % n) for i in range(n)])  11.3 us
    ppermute x6, starting transfers between devices, z_up(): return lax.ppermute(v, 'dp', [(i, (i + 4) % n) for i in range(n)])  8.16 us
  transfers between devices with their start and end apart: 80, of which 38 were waited for; matrix products, arithmetic and copies ran while one was open for 4% of the time, Pallas kernels for 23%

commit v1 on v0

--- a/solution.py
+++ b/solution.py
@@ -158,7 +158,7 @@
     ("x0", "y0", "s1"),
     ("d0", "e0", "x1", "y1", "s2"),
     ("d1", "e1", "x2", "y2", "s3"),
-    ("d2", "e2", "x3", "y3"),
+    ("f2", "x3", "y3"),
     ("d3", "e3"),
 )
 
@@ -173,24 +173,29 @@
         sources = {}
         for name in tasks:
             kind, k = name[0], int(name[1])
-            sources[name] = {"s": f"s{k - 1}", "x": f"s{k}", "y": f"s{k}", "d": f"x{k}", "e": f"y{k}"}[kind]
+            sources[name] = {"s": f"s{k - 1}", "x": f"s{k}", "y": f"s{k}", "d": f"x{k}", "e": f"y{k}", "f": f"x{k}"}[kind]
+        if "y3" in sources:
+            sources["y3"] = "y2"
         names = list(dict.fromkeys([*sources.values(), *across]))
         if r:
             have.update(zip(names, fence([have[i] for i in names])))
         for name, source in sources.items():
             move = {
-                "s": z_up, "x": x_flip, "y": y_flip, "d": lambda v: y_flip(v[:SEND_ONE]), "e": lambda v: x_flip(v[SEND_ONE:])
+                "s": z_up, "x": x_flip, "y": y_flip, "f": y_flip, "d": lambda v: y_flip(v[:SEND_ONE]), "e": lambda v: x_flip(v[SEND_ONE:])
             }[name[0]]
-            have[name] = move(have[source])
-        if 0 < r < 4:
+            have[name] = z_up(have[source]) if name == "y3" else move(have[source])
+        if r in (1, 2):
             names = [*across, *tasks[:2]]
             have.update(zip(names, fence([have[i] for i in names])))
         for i in across:
             have["c" + i] = core_flip(have[i])
         across = list(tasks)
+    names = ["cs3", "cx3", "cy3", *across]
+    have.update(zip(names, fence([have[i] for i in names])))
     for i in across:
         have["c" + i] = core_flip(have[i])
-    return [[have[c + kind + str(k)] for c in ("", "c") for k in range(4) for kind in kinds] for kinds in ("sxyd", "sxye")]
+    orders = [["sxy" + (last if k != 2 else "f") for k in range(4)] for last in "de"]
+    return [[have[c + kind + str(k)] for c in ("", "c") for k in range(4) for kind in kinds[k]] for kinds in orders]
 
 
 def add16(a, b):
@@ -256,7 +261,7 @@
         made = []
         for other in (0, 1):
             for kind in range(4):
-                source = pieces[16 * other + 4 * k + kind].at[pl.ds(SEND_ONE if block and kind < 3 else 0, 288)]
+                source = pieces[16 * other + 4 * k + kind].at[pl.ds(SEND_ONE if block and (kind < 3 or k == 2) else 0, 288)]
                 rows = pl.ds(pl.multiple_of(288 * owner(info, plane, kind, other), 16), 288)
                 made.append(pltpu.make_async_copy(source, wbuf.at[rows], sem.at[8 * plane + 2 * kind + other]))
         return made
@@ -328,7 +333,7 @@
     info, u_ref, *refs
 ):
     pieces = diagonals = refs[:32]
-    y_out, xh1_o, rs1_o, xh2_o, rs2_o, gp_o, e_o, h_o, att_o, u_o, q_o, pu_o, qk_o, p_o, vec, vbuf, wflat, w1, sem = refs[32:]
+    y_out, cls_out, xh1_o, rs1_o, xh2_o, rs2_o, gp_o, e_o, h_o, att_o, u_o, q_o, pu_o, qk_o, p_o, vec, vbuf, wflat, w1, sem = refs[32:]
     wait_vecs, wait = fill(info, pieces, diagonals, 0, wflat, vbuf, sem)
     wbuf = wflat.reshape(GRANS, GRAN, D)
     start = info[5]
@@ -373,7 +378,9 @@
     xhat, rstd = norm_forward(h + f)
     xh2_o[...] = xhat
     rs2_o[...] = jnp.broadcast_to(rstd, (16, 128))
-    y_out[...] = xhat * vec[V_G2 : V_G2 + 1, :] + vec[V_C2 : V_C2 + 1, :]
+    y = xhat * vec[V_G2 : V_G2 + 1, :] + vec[V_C2 : V_C2 + 1, :]
+    y_out[...] = y
+    cls_out[...] = y[0:2, :].astype(BF16)
     h_o[...] = h16
     att_o[...] = att
     u_o[...] = cls16
@@ -590,7 +597,7 @@
             for kind in range(4):
                 i = 16 * other + 4 * k + kind
                 dev = owner(info, (info[1] + 4 - k) & 3, kind, other)
-                source = pieces[i].at[pl.ds(SEND_ONE if kind < 3 else 0, 288)]
+                source = pieces[i].at[pl.ds(SEND_ONE if kind < 3 or k == 2 else 0, 288)]
                 rows = pl.ds(pl.multiple_of(288 * jnp.minimum(dev, 15), 16), 288)
                 copy = pltpu.make_async_copy(source, wflat.at[rows], sem.at[i])
                 used = dev < 11
@@ -845,13 +852,13 @@
         pltpu.VMEM((GRANS * GRAN, D), BF16),
         pltpu.VMEM((4, D, D), BF16),
     ]
-    y_cls, *saved = call(
+    y_cls, cls, *saved = call(
         first_forward,
         "first_forward",
         (info, u, *pieces0),
         [SMEM, VMEM] + [ANY] * 32,
-        (row, *saved_shapes),
-        (VMEM,) * 14,
+        (row, struct(2, D, dtype=BF16), *saved_shapes),
+        (VMEM,) * 15,
         weights + [pltpu.SemaphoreType.DMA((64,))],
         flops=2 * 32 * PL,
         moved=2 * PL,
@@ -909,7 +916,7 @@
             name="total",
         )(mine, came, over_x, over_y, last_x, last_y)
 
-    cls = gather_step(y_cls[0:2].astype(BF16), 0, device)()
+    cls = gather_step(cls, 0, device)()
     theirs_a1, theirs_a2, cls = fence([theirs_a1, theirs_a2, cls])
     came_a1, came_a2 = core_flip(theirs_a1), core_flip(theirs_a2)
     cls = gather_step(cls, 1, device)()

time: 353 us -> 341 us (0.966)
  waiting for transfers between devices: 168 us -> 160 us
    ppermute x67 -> x64, waiting for transfers between devices: 154 us -> 142 us  [flip(): lax.ppermute(v, axis, [(i, i ^ bit) for i in range(lax.axis_size(axis))])]
    ppermute x6 -> x7, waiting for transfers between devices: 11.3 us -> 14.9 us  [z_up(): return lax.ppermute(v, 'dp', [(i, (i + 4) % n) for i in range(n)])]
    ppermute x6 -> x7, starting transfers between devices: 8.16 us -> 5.66 us  [z_up(): return lax.ppermute(v, 'dp', [(i, (i + 4) % n) for i in range(n)])]
    ppermute x67 -> x64, starting transfers between devices: 45 us -> 44.6 us  [flip(): lax.ppermute(v, axis, [(i, i ^ bit) for i in range(lax.axis_size(axis))])]
  transfers between devices with their start and end apart: 80 -> 78, of which waited for: 38 -> 41; matrix products, arithmetic and copies ran while one was open for 4% -> 4% of each run, Pallas kernels for 23% -> 24%
where the time goes in v1:
time: 341 us; the launch traced here: 338 us
  waiting for transfers between devices  160 us (47%)
  Pallas kernels  92 us (27%)
  starting transfers between devices  59.1 us (17%)
  other arithmetic  16.5 us (5%)
  local copies, waits for them, and re-layouts  9.18 us (3%)
    ppermute x64, waiting for transfers between devices, flip(): lax.ppermute(v, axis, [(i, i ^ bit) for i in range(lax.axis_size(axis))])  142 us
    pallas_call x7, Pallas kernels, call(): pl.pallas_call(kernel, out_shape=outs, in_specs=in_specs, out_specs=out_s...  78 us
    ppermute x64, starting transfers between devices, flip(): lax.ppermute(v, axis, [(i, i ^ bit) for i in range(lax.axis_size(axis))])  44.6 us
    ppermute x7, waiting for transfers between devices, z_up(): return lax.ppermute(v, 'dp', [(i, (i + 4) % n) for i in range(n)])  14.9 us
  transfers between devices with their start and end apart: 78, of which 41 were waited for; matrix products, arithmetic and copies ran while one was open for 4% of the time, Pallas kernels for 24%

profile of v1, /device:TPU:0, one launch (start us, length us, event | category | flops | bytes accessed | tf_op | source)
XLA Modules:
  0.0 338.3 jit_solution(16854764779193872754)
XLA Ops:
  11.0 16.9 %collective-permute-done.refs_1_ = bf16[592,768]{1,0:T(8,128)(2,1)S(1)} collective-permute-done((bf16[592,768]{1,0:T(8,128)(2,1)}, bf16[592,768]{1,0:T(8,128)(2,1)S(1)}, u32[]{:S(2)}, u32[]{:S(2)}) %collective-permute-start) | collective-permute-done | bytes 909344 | tf_op jit(solution)/shard_map/ppermute | solution.py:98
  29.4 3.1 collective-permute-done.2.refs_4_
  36.9 25.7 %collective-permute-done.4.refs_3_ = bf16[288,768]{1,0:T(8,128)(2,1)} collective-permute-done((bf16[288,768]{1,0:T(8,128)(2,1)S(1)}, bf16[288,768]{1,0:T(8,128)(2,1)}, u32[]{:S(2)}, u32[]{:S(2)}) %collective-permute-start.4) | collective-permute-done | bytes 442400 | tf_op jit(solution)/shard_map/ppermute | solution.py:98
  68.0 8.6 %collective-permute-done.9.refs_7_ = bf16[288,768]{1,0:T(8,128)(2,1)} collective-permute-done((bf16[288,768]{1,0:T(8,128)(2,1)S(1)}, bf16[288,768]{1,0:T(8,128)(2,1)}, u32[]{:S(2)}, u32[]{:S(2)}) %collective-permute-start.9) | collective-permute-done | bytes 442400 | tf_op jit(solution)/shard_map/ppermute | solution.py:98
  78.7 13.7 %collective-permute-done.10.refs_9_ = bf16[592,768]{1,0:T(8,128)(2,1)S(1)} collective-permute-done((bf16[592,768]{1,0:T(8,128)(2,1)S(1)}, bf16[592,768]{1,0:T(8,128)(2,1)S(1)}, u32[]{:S(2)}, u32[]{:S(2)}) %collective-permute-start.10) | collective-permute-done | bytes 909344 | tf_op jit(solution)/shard_map/ppermute | solution.py:98
  97.3 17.7 %collective-permute-done.13.refs_13_ = bf16[592,768]{1,0:T(8,128)(2,1)S(1)} collective-permute-done((bf16[592,768]{1,0:T(8,128)(2,1)S(1)}, bf16[592,768]{1,0:T(8,128)(2,1)S(1)}, u32[]{:S(2)}, u32[]{:S(2)}) %collective-permute-start.13) | collective-permute-done | bytes 909344 | tf_op jit(solution)/shard_map/ppermute | solution.py:98
  115.0 3.3 collective-permute-done.14.refs_14_
  123.1 11.0 %collective-permute-done.20.refs_15_ = bf16[288,768]{1,0:T(8,128)(2,1)} collective-permute-done((bf16[288,768]{1,0:T(8,128)(2,1)S(1)}, bf16[288,768]{1,0:T(8,128)(2,1)}, u32[]{:S(2)}, u32[]{:S(2)}) %collective-permute-start.20) | collective-permute-done | bytes 442400 | tf_op jit(solution)/shard_map/ppermute | solution.py:98
  143.3 9.6 %first_forward.1 = (f32[16,768]{1,0:T(8,128)}, bf16[2,768]{1,0:T(2,128)(2,1)}, f32[16,768]{1,0:T(8,128)}, f32[16,128]{1,0:T(8,128)}, f32[16,768]{1,0:T(8,128)}, ...) custom-call(s32[8]{0:T(128)} %stack.23.info, ...), custom_call_target="tpu_custom_call" | custom-call | flops 452984832 | bytes 14155776 | tf_op jit(solution)/shard_map/first_forward/pallas_call | solution.py:811
  155.1 23.7 %second_block.1 = (bf16[256,768]{1,0:T(8,128)(2,1)}, f32[256,768]{1,0:T(8,128)}, f32[16,768]{1,0:T(8,128)}, bf16[256,768]{1,0:T(8,128)(2,1)}, bf16[256,768]{1,0:...) custom-call(s32[8]{0:T(128)} %stack.23.info, ...), custom_call_target="tpu_custom_call" | custom-call | flops 7247757312 | bytes 28311552 | tf_op jit(solution)/shard_map/second_block/pallas_call | solution.py:811
  192.1 14.4 %second_attention.1 = (f32[256,768]{1,0:T(8,128)}, f32[16,768]{1,0:T(8,128)}, bf16[1152,768]{1,0:T(8,128)(2,1)}, bf16[1152,768]{1,0:T(8,128)(2,1)}, bf16[1152,76...) custom-call(s32[8]{0:T(128)} %stack.23.info, f32[256,768]{1,0:T(8,128)} %get-tuple-element.165.dr, ...), custom_call_target="tpu_custom_call" | custom-call | flops 3623878656 | bytes 14155776 | tf_op jit(solution)/shard_map/second_attention/pallas_call | solution.py:811
  206.5 3.5 %collective-permute-done.45.over_y = bf16[576,768]{1,0:T(8,128)(2,1)} collective-permute-done((bf16[576,768]{1,0:T(8,128)(2,1)}, bf16[576,768]{1,0:T(8,128)(2,1)}, u32[]{:S(2)}, u32[]{:S(2)}) %collective-permute-start.45) | collective-permute-done | bytes 884768 | tf_op jit(solution)/shard_map/ppermute | solution.py:98
  213.6 3.7 %collective-permute-done.48 = bf16[1152,768]{1,0:T(8,128)(2,1)S(1)} collective-permute-done((bf16[1152,768]{1,0:T(8,128)(2,1)S(1)}, bf16[1152,768]{1,0:T(8,128)(2,1)S(1)}, u32[]{:S(2)}, u32[]{:S(2)}) %collective-permute-start.48) | collective-permute-done | bytes 1769504 | tf_op jit(solution)/shard_map/ppermute | solution.py:98
  222.6 4.0 %collective-permute-done.47 = bf16[32,768]{1,0:T(8,128)(2,1)S(1)} collective-permute-done((bf16[32,768]{1,0:T(8,128)(2,1)}, bf16[32,768]{1,0:T(8,128)(2,1)S(1)}, u32[]{:S(2)}, u32[]{:S(2)}) %collective-permute-start.47) | collective-permute-done | bytes 49184 | tf_op jit(solution)/shard_map/ppermute | solution.py:98
  229.7 14.5 %first_backward.1 = (f32[256,768]{1,0:T(8,128)}, bf16[96,768]{1,0:T(8,128)(2,1)}, f32[1,1]{1,0:T(1,128)}) custom-call(s32[8]{0:T(128)} %stack.23.info, bf16[256,768]{1,0:T(8,128)(2,1)} %bitcast.47, bf16[64,768]{1,0:T(8,128)(2,1)} %pad_maximum_fusion.cls_all, f32[256,768]{1,0:T(8,128)} %get-tuple-element.182.dz, f32[16,768]{1,0:T(8,128)} %get-tuple-element.183.vg1, ...), custom_call_target="tpu_custom_call" | custom-call | flops 452984832 | bytes 14155776 | tf_op jit(solution)/shard_map/first_backward/pallas_call | solution.py:811
  247.3 3.9 %collective-permute-done.52.last_x = bf16[288,768]{1,0:T(8,128)(2,1)S(1)} collective-permute-done((bf16[288,768]{1,0:T(8,128)(2,1)}, bf16[288,768]{1,0:T(8,128)(2,1)S(1)}, u32[]{:S(2)}, u32[]{:S(2)}) %collective-permute-start.52) | collective-permute-done | bytes 442400 | tf_op jit(solution)/shard_map/ppermute | solution.py:98
  258.7 3.2 total.1
  264.5 4.3 %order.1 = (bf16[288,768]{1,0:T(8,128)(2,1)}, bf16[288,768]{1,0:T(8,128)(2,1)}, bf16[288,768]{1,0:T(8,128)(2,1)}, bf16[288,768]{1,0:T(8,128)(2,1)}) custom-call(s32[8]{0:T(128)} %stack.23.info, bf16[288,768]{1,0:T(8,128)(2,1)} %get-tuple-element.210.a3, bf16[288,768]{1,0:T(8,128)(2,1)} %get-tuple-element.211.a2, bf16[1152,768]{1,0:T(8,128)(2,1)} %get-tuple-element.199.mine, ...), custom_call_target="tpu_custom_call" | custom-call | tf_op jit(solution)/shard_map/order/pallas_call | solution.py:974
  272.6 8.5 %collective-permute-done.68 = bf16[288,768]{1,0:T(8,128)(2,1)S(1)} collective-permute-done((bf16[288,768]{1,0:T(8,128)(2,1)}, bf16[288,768]{1,0:T(8,128)(2,1)S(1)}, u32[]{:S(2)}, u32[]{:S(2)}) %collective-permute-start.68) | collective-permute-done | bytes 442400 | tf_op jit(solution)/shard_map/ppermute | solution.py:115
  287.0 3.8 %collective-permute-done.59.refs_3_ = bf16[192,768]{1,0:T(8,128)(2,1)} collective-permute-done((bf16[192,768]{1,0:T(8,128)(2,1)S(1)}, bf16[192,768]{1,0:T(8,128)(2,1)}, u32[]{:S(2)}, u32[]{:S(2)}) %collective-permute-start.59) | collective-permute-done | bytes 294944 | tf_op jit(solution)/shard_map/ppermute | solution.py:98
  290.8 3.9 %collective-permute-done.60.refs_4_ = bf16[192,768]{1,0:T(8,128)(2,1)} collective-permute-done((bf16[192,768]{1,0:T(8,128)(2,1)S(1)}, bf16[192,768]{1,0:T(8,128)(2,1)}, u32[]{:S(2)}, u32[]{:S(2)}) %collective-permute-start.60) | collective-permute-done | bytes 294944 | tf_op jit(solution)/shard_map/ppermute | solution.py:98
  298.7 10.1 %owner_grad.1 = (f32[1728,128]{1,0:T(8,128)}, f32[24,768]{1,0:T(8,128)}) custom-call(s32[8]{0:T(128)} %stack.23.info, bf16[384,768]{1,0:T(8,128)(2,1)} %copy-done.36, bf16[384,768]{1,0:T(8,128)(2,1)} %copy-done.34, bf16[384,768]{1,0:T(8,128)(2,1)} %copy-done.35, bf16[192,768]{1,0:T(8,128)(2,1)} %collective-permute-done.59.refs_3_, ...), custom_call_target="tpu_custom_call" | custom-call | flops 905969664 | bytes 4718592 | tf_op jit(solution)/shard_map/owner_grad/pallas_call | solution.py:811
  311.1 3.2 join_grads.1
  331.3 6.5 %adamw.1 = (f32[3456,128]{1,0:T(8,128)}, f32[3456,128]{1,0:T(8,128)}, f32[3456,128]{1,0:T(8,128)}, f32[2,288]{1,0:T(2,128)}, f32[2,288]{1,0:T(2,128)}, /*index=5*/f32[2,288]{1,0:T(2,128)}, f32[1,1]{1,0:T(1,128)}) custom-call(f32[8,128]{1,0:T(8,128)} %add_add_fusion.sq, f32[3456,128]{1,0:T(8,128)} %bitcast.44, f32[3456,128]{1,0:T(8,128)} %bitcast.48, ...), custom_call_target="tpu_custom_call" | custom-call | tf_op jit(solution)/shard_map/adamw/pallas_call | solution.py:1020
  (267 shorter events, 115.8 us)
Async XLA Ops:
  4.6 23.4 %collective-permute-start = (bf16[592,768]{1,0:T(8,128)(2,1)}, bf16[592,768]{1,0:T(8,128)(2,1)S(1)}, u32[]{:S(2)}, u32[]{:S(2)}) collective-permute-start(bf16[592,768]{1,0:T(8,128)(2,1)} %pack.1.refs_0_), channel_id=1, source_target_pairs={{0,4},{2,6},{4,0},{6,2},{8,12},{10,14},{12,8},{14,10},{16,20},{18,... | collective-permute-start | bytes 2727944 | tf_op jit(solution)/shard_map/ppermute | solution.py:98
  7.5 21.8 %collective-permute-start.1 = (bf16[592,768]{1,0:T(8,128)(2,1)}, bf16[592,768]{1,0:T(8,128)(2,1)S(1)}, u32[]{:S(2)}, u32[]{:S(2)}) collective-permute-start(bf16[592,768]{1,0:T(8,128)(2,1)} %pack.1.refs_0_), channel_id=1, source_target_pairs={{0,1},{1,0},{2,3},{3,2},{4,5},{5,4},{6,7},{7,6},{8,9},{9,8},{10,11... | collective-permute-start | bytes 2727944 | tf_op jit(solution)/shard_map/ppermute | solution.py:98
  9.0 23.5 %collective-permute-start.2 = (bf16[592,768]{1,0:T(8,128)(2,1)}, bf16[592,768]{1,0:T(8,128)(2,1)S(1)}, u32[]{:S(2)}, u32[]{:S(2)}) collective-permute-start(bf16[592,768]{1,0:T(8,128)(2,1)} %pack.1.refs_0_), channel_id=1, source_target_pairs={{0,8},{2,10},{4,12},{6,14},{8,16},{10,18},{12,20},{14,22},{16,24},... | collective-permute-start | bytes 2727944 | tf_op jit(solution)/shard_map/ppermute | solution.py:115
  32.5 30.8 %collective-permute-start.5 = (bf16[592,768]{1,0:T(8,128)(2,1)S(1)}, bf16[592,768]{1,0:T(8,128)(2,1)S(1)}, u32[]{:S(2)}, u32[]{:S(2)}) collective-permute-start(bf16[592,768]{1,0:T(8,128)(2,1)S(1)} %collective-permute-done.2.refs_4_), channel_id=1, source_target_pairs={{0,4},{2,6},{4,0},{6,2},{8,12},{10,14},{12,8},{14,10},{16,20},{18,... | collective-permute-start | bytes 2727944 | tf_op jit(solution)/shard_map/ppermute | solution.py:98
  33.0 30.3 %collective-permute-start.6 = (bf16[592,768]{1,0:T(8,128)(2,1)S(1)}, bf16[592,768]{1,0:T(8,128)(2,1)S(1)}, u32[]{:S(2)}, u32[]{:S(2)}) collective-permute-start(bf16[592,768]{1,0:T(8,128)(2,1)S(1)} %collective-permute-done.2.refs_4_), channel_id=1, source_target_pairs={{0,1},{1,0},{2,3},{3,2},{4,5},{5,4},{6,7},{7,6},{8,9},{9,8},{10,11... | collective-permute-start | bytes 2727944 | tf_op jit(solution)/shard_map/ppermute | solution.py:98
  33.5 29.8 %collective-permute-start.7 = (bf16[592,768]{1,0:T(8,128)(2,1)S(1)}, bf16[592,768]{1,0:T(8,128)(2,1)S(1)}, u32[]{:S(2)}, u32[]{:S(2)}) collective-permute-start(bf16[592,768]{1,0:T(8,128)(2,1)S(1)} %collective-permute-done.2.refs_4_), channel_id=1, source_target_pairs={{0,8},{2,10},{4,12},{6,14},{8,16},{10,18},{12,20},{14,22},{16,24},... | collective-permute-start | bytes 2727944 | tf_op jit(solution)/shard_map/ppermute | solution.py:115
  33.6 29.7 %collective-permute-start.3 = (bf16[304,768]{1,0:T(8,128)(2,1)S(1)}, bf16[304,768]{1,0:T(8,128)(2,1)S(1)}, u32[]{:S(2)}, u32[]{:S(2)}) collective-permute-start(bf16[304,768]{1,0:T(8,128)(2,1)S(1)} %slice.88), channel_id=1, source_target_pairs={{0,1},{1,0},{2,3},{3,2},{4,5},{5,4},{6,7},{7,6},{8,9},{9,8},{10,11... | collective-permute-start | bytes 1400840 | tf_op jit(solution)/shard_map/ppermute | solution.py:98
  35.3 27.3 %collective-permute-start.4 = (bf16[288,768]{1,0:T(8,128)(2,1)S(1)}, bf16[288,768]{1,0:T(8,128)(2,1)}, u32[]{:S(2)}, u32[]{:S(2)}) collective-permute-start(bf16[288,768]{1,0:T(8,128)(2,1)S(1)} %slice.89), channel_id=1, source_target_pairs={{0,4},{2,6},{4,0},{6,2},{8,12},{10,14},{12,8},{14,10},{16,20},{18,... | collective-permute-start | bytes 1327112 | tf_op jit(solution)/shard_map/ppermute | solution.py:98
  65.5 26.8 %collective-permute-start.10 = (bf16[592,768]{1,0:T(8,128)(2,1)S(1)}, bf16[592,768]{1,0:T(8,128)(2,1)S(1)}, u32[]{:S(2)}, u32[]{:S(2)}) collective-permute-start(bf16[592,768]{1,0:T(8,128)(2,1)S(1)} %collective-permute-done.7.refs_8_), channel_id=1, source_target_pairs={{0,4},{2,6},{4,0},{6,2},{8,12},{10,14},{12,8},{14,10},{16,20},{18,... | collective-permute-start | bytes 2727944 | tf_op jit(solution)/shard_map/ppermute | solution.py:98
  66.3 26.1 %collective-permute-start.11 = (bf16[592,768]{1,0:T(8,128)(2,1)S(1)}, bf16[592,768]{1,0:T(8,128)(2,1)S(1)}, u32[]{:S(2)}, u32[]{:S(2)}) collective-permute-start(bf16[592,768]{1,0:T(8,128)(2,1)S(1)} %collective-permute-done.7.refs_8_), channel_id=1, source_target_pairs={{0,8},{2,10},{4,12},{6,14},{8,16},{10,18},{12,20},{14,22},{16,24},... | collective-permute-start | bytes 2727944 | tf_op jit(solution)/shard_map/ppermute | solution.py:115
  66.7 27.5 %collective-permute-start.12 = (bf16[592,768]{1,0:T(8,128)(2,1)S(1)}, bf16[592,768]{1,0:T(8,128)(2,1)S(1)}, u32[]{:S(2)}, u32[]{:S(2)}) collective-permute-start(bf16[592,768]{1,0:T(8,128)(2,1)S(1)} %collective-permute-done.7.refs_8_), channel_id=1, source_target_pairs={{0,1},{1,0},{2,3},{3,2},{4,5},{5,4},{6,7},{7,6},{8,9},{9,8},{10,11... | collective-permute-start | bytes 2727944 | tf_op jit(solution)/shard_map/ppermute | solution.py:98
  94.7 23.6 %collective-permute-start.14 = (bf16[592,768]{1,0:T(8,128)(2,1)S(1)}, bf16[592,768]{1,0:T(8,128)(2,1)S(1)}, u32[]{:S(2)}, u32[]{:S(2)}) collective-permute-start(bf16[592,768]{1,0:T(8,128)(2,1)S(1)} %collective-permute-done.12.refs_10_), channel_id=1, source_target_pairs={{0,8},{2,10},{4,12},{6,14},{8,16},{10,18},{12,20},{14,22},{16,24},... | collective-permute-start | bytes 2727944 | tf_op jit(solution)/shard_map/ppermute | solution.py:115
  95.8 22.5 %collective-permute-start.15 = (bf16[592,768]{1,0:T(8,128)(2,1)S(1)}, bf16[592,768]{1,0:T(8,128)(2,1)S(1)}, u32[]{:S(2)}, u32[]{:S(2)}) collective-permute-start(bf16[592,768]{1,0:T(8,128)(2,1)S(1)} %collective-permute-done.10.refs_9_), channel_id=1, source_target_pairs={{0,1},{1,0},{2,3},{3,2},{4,5},{5,4},{6,7},{7,6},{8,9},{9,8},{10,11... | collective-permute-start | bytes 2727944 | tf_op jit(solution)/shard_map/ppermute | solution.py:98
  96.8 22.0 %collective-permute-start.25 = (bf16[592,768]{1,0:T(8,128)(2,1)S(1)}, bf16[592,768]{1,0:T(8,128)(2,1)S(1)}, u32[]{:S(2)}, u32[]{:S(2)}) collective-permute-start(bf16[592,768]{1,0:T(8,128)(2,1)S(1)} %collective-permute-done.2.refs_4_), channel_id=1, source_target_pairs={{0,2},{2,0},{4,6},{6,4},{8,10},{10,8},{12,14},{14,12},{16,18},{18,... | collective-permute-start | bytes 2727944 | tf_op jit(solution)/shard_map/ppermute | solution.py:98
  96.8 25.2 %collective-permute-start.26 = (bf16[592,768]{1,0:T(8,128)(2,1)S(1)}, bf16[592,768]{1,0:T(8,128)(2,1)S(1)}, u32[]{:S(2)}, u32[]{:S(2)}) collective-permute-start(bf16[592,768]{1,0:T(8,128)(2,1)S(1)} %collective-permute-done.5.refs_5_), channel_id=1, source_target_pairs={{0,2},{2,0},{4,6},{6,4},{8,10},{10,8},{12,14},{14,12},{16,18},{18,... | collective-permute-start | bytes 2727944 | tf_op jit(solution)/shard_map/ppermute | solution.py:98
  152.9 25.9 %collective-permute-start.37 = (bf16[2,768]{1,0:T(2,128)(2,1)}, bf16[2,768]{1,0:T(2,128)(2,1)S(1)}, u32[]{:S(2)}, u32[]{:S(2)}) collective-permute-start(bf16[2,768]{1,0:T(2,128)(2,1)} %get-tuple-element.157), channel_id=1, source_target_pairs={{0,1},{1,0},{2,3},{3,2},{4,5},{5,4},{6,7},{7,6},{8,9},{9,8},{10,11... | collective-permute-start | bytes 9224 | tf_op jit(solution)/shard_map/ppermute | solution.py:127
  154.5 24.3 %collective-permute-start.38 = (bf16[2,768]{1,0:T(2,128)(2,1)}, bf16[2,768]{1,0:T(2,128)(2,1)S(1)}, u32[]{:S(2)}, u32[]{:S(2)}) collective-permute-start(bf16[2,768]{1,0:T(2,128)(2,1)} %get-tuple-element.157), channel_id=1, source_target_pairs={{0,2},{2,0},{4,6},{6,4},{8,10},{10,8},{12,14},{14,12},{16,18},{18,... | collective-permute-start | bytes 9224 | tf_op jit(solution)/shard_map/ppermute | solution.py:98
  154.5 24.3 %collective-permute-start.39 = (bf16[2,768]{1,0:T(2,128)(2,1)}, bf16[2,768]{1,0:T(2,128)(2,1)S(1)}, u32[]{:S(2)}, u32[]{:S(2)}) collective-permute-start(bf16[2,768]{1,0:T(2,128)(2,1)} %get-tuple-element.157), channel_id=1, source_target_pairs={{0,3},{1,2},{2,1},{3,0},{4,7},{5,6},{6,5},{7,4},{8,11},{9,10},{10,... | collective-permute-start | bytes 9224 | tf_op jit(solution)/shard_map/ppermute | solution.py:127
  179.0 27.6 %collective-permute-start.40 = (bf16[1152,768]{1,0:T(8,128)(2,1)}, bf16[1152,768]{1,0:T(8,128)(2,1)S(1)}, u32[]{:S(2)}, u32[]{:S(2)}) collective-permute-start(bf16[1152,768]{1,0:T(8,128)(2,1)} %get-tuple-element.158), channel_id=1, source_target_pairs={{0,2},{2,0},{4,6},{6,4},{8,10},{10,8},{12,14},{14,12},{16,18},{18,... | collective-permute-start | bytes 5308424 | tf_op jit(solution)/shard_map/ppermute | solution.py:98
  219.0 25.2 %collective-permute-start.49 = (bf16[1152,768]{1,0:T(8,128)(2,1)}, bf16[1152,768]{1,0:T(8,128)(2,1)S(1)}, u32[]{:S(2)}, u32[]{:S(2)}) collective-permute-start(bf16[1152,768]{1,0:T(8,128)(2,1)} %get-tuple-element.200), channel_id=1, source_target_pairs={{0,2},{2,0},{4,6},{6,4},{8,10},{10,8},{12,14},{14,12},{16,18},{18,... | collective-permute-start | bytes 5308424 | tf_op jit(solution)/shard_map/ppermute | solution.py:98
  219.1 25.1 %collective-permute-start.50 = (bf16[576,768]{1,0:T(8,128)(2,1)}, bf16[576,768]{1,0:T(8,128)(2,1)}, u32[]{:S(2)}, u32[]{:S(2)}) collective-permute-start(bf16[576,768]{1,0:T(8,128)(2,1)} %get-tuple-element.201), channel_id=1, source_target_pairs={{0,1},{1,0},{2,3},{3,2},{4,5},{5,4},{6,7},{7,6},{8,9},{9,8},{10,11... | collective-permute-start | bytes 2654216 | tf_op jit(solution)/shard_map/ppermute | solution.py:98
  219.9 24.3 %collective-permute-start.51 = (bf16[576,768]{1,0:T(8,128)(2,1)}, bf16[576,768]{1,0:T(8,128)(2,1)}, u32[]{:S(2)}, u32[]{:S(2)}) collective-permute-start(bf16[576,768]{1,0:T(8,128)(2,1)} %get-tuple-element.202), channel_id=1, source_target_pairs={{0,4},{2,6},{4,0},{6,2},{8,12},{10,14},{12,8},{14,10},{16,20},{18,... | collective-permute-start | bytes 2654216 | tf_op jit(solution)/shard_map/ppermute | solution.py:98
  221.7 29.5 %collective-permute-start.52 = (bf16[288,768]{1,0:T(8,128)(2,1)}, bf16[288,768]{1,0:T(8,128)(2,1)S(1)}, u32[]{:S(2)}, u32[]{:S(2)}) collective-permute-start(bf16[288,768]{1,0:T(8,128)(2,1)} %get-tuple-element.204), channel_id=1, source_target_pairs={{0,4},{2,6},{4,0},{6,2},{8,12},{10,14},{12,8},{14,10},{16,20},{18,... | collective-permute-start | bytes 1327112 | tf_op jit(solution)/shard_map/ppermute | solution.py:98
  226.7 24.5 %collective-permute-start.53 = (bf16[288,768]{1,0:T(8,128)(2,1)}, bf16[288,768]{1,0:T(8,128)(2,1)}, u32[]{:S(2)}, u32[]{:S(2)}) collective-permute-start(bf16[288,768]{1,0:T(8,128)(2,1)} %get-tuple-element.205), channel_id=1, source_target_pairs={{0,1},{1,0},{2,3},{3,2},{4,5},{5,4},{6,7},{7,6},{8,9},{9,8},{10,11... | collective-permute-start | bytes 1327112 | tf_op jit(solution)/shard_map/ppermute | solution.py:98
  (101 other events, 1661.1 us)

commit v2 on v1

--- a/solution.py
+++ b/solution.py
@@ -27,7 +27,7 @@
 TOK = 256
 GRAN = 96
 GRANS = PL // D // GRAN
-VMEM_BYTES = 63_000_000
+VMEM_BYTES = 66_400_000
 
 V_BQ, V_BV, V_BO, V_G1, V_C1, V_B1, V_B2, V_G2, V_C2 = 0, 1, 2, 3, 4, 5, 9, 10, 11
 
@@ -147,7 +147,7 @@
     for bits in SUM_STEPS:
         got = [v] + [xor_flip(v, *b) for b in bits]
         v = got[0] + got[1] if len(got) == 2 else (got[0] + got[1]) + (got[2] + got[3])
-    return v
+    return got
 
 
 def pick(index, cases):
@@ -491,9 +491,10 @@
 def second_block(info, u_ref, cot_ref, y_ref, *refs):
     pieces = refs[:32]
     diagonals = {4 * i + 3: refs[32 + i] for i in range(8)}
-    head_out, dr_out, vg_out, zb, qs, ks, vs, att = refs[40:48]
+    head_out, dr_out, vg_out = refs[40:43]
+    mids_out = refs[43:48]
     pm_out, w1_grad, theirs1, theirs2, mine1, mine2 = refs[48:54]
-    (vec, vbuf, wflat, w1, grads, zf, pm, xh1, hb, ht, gp, es, das, xh2, acc, stage, dfs, sem, osem) = refs[54:]
+    (vec, vbuf, wflat, w1, grads, zf, pm, xh1, hb, ht, gp, es, das, xh2, acc, stage, dfs, zb, qs, ks, vs, att, sem, osem) = refs[54:]
     wait_vecs, wait = fill(info, pieces, diagonals, 1, wflat, vbuf, sem)
     wbuf = wflat.reshape(GRANS, GRAN, D)
     gbuf = grads.reshape(GRANS, GRAN, D)
@@ -527,7 +528,10 @@
 
     lax.fori_loop(0, 6, attend, 0, unroll=True)
     saved = [pltpu.make_async_copy(pm, pm_out, osem.at[28])]
-    saved[0].start()
+    for i, (source, out) in enumerate(zip((zb, qs, ks, vs, att), mids_out)):
+        saved.append(pltpu.make_async_copy(source, out, osem.at[30 + i]))
+    for copy in saved:
+        copy.start()
     wait(1)
     xhat, rstd1 = norm_forward(zf[...] + (nn(att[...], w_out(wbuf)) + vec[V_BO : V_BO + 1, :]))
     xh1[...] = xhat
@@ -774,8 +778,8 @@
         by_kind(3 * info[0] + gi, emit)
 
 
-def adamw_kernel(sq, w, m, v, g, vw, vm, vv, vg, w_new, m_new, v_new, vw_new, vm_new, vv_new, norm_out):
-    norm = jnp.sqrt(sq[...])
+def adamw_kernel(sq0, sq1, sq2, sq3, w, m, v, g, vw, vm, vv, vg, w_new, m_new, v_new, vw_new, vm_new, vv_new, norm_out):
+    norm = jnp.sqrt((sq0[...] + sq1[...]) + (sq2[...] + sq3[...]))
     norm_out[0, 0] = norm[0, 0]
     coef = jnp.minimum(1.0, math.sqrt(2 * (PL + QL)) / (norm[0:1, 0:1] + 1e-06))
     w_new[...], m_new[...], v_new[...] = adamw_update(w[...], m[...], v[...], g[...] * coef, 0.1, weight_decay)
@@ -838,7 +842,7 @@
     u = tokens[0]
     cot = cotangent[0]
     flat = flat_view(mats)
-    own = call(pack_kernel, "pack", (info, flat, vecs), [SMEM, VMEM, VMEM], struct(SEND, D, dtype=BF16), VMEM)
+    own = call(pack_kernel, "pack", (device.reshape(1), flat, vecs), [SMEM, VMEM, VMEM], struct(SEND, D, dtype=BF16), VMEM)
     pieces0, pieces1 = gather_blocks(own)
     row = struct(16, D)
     row16 = struct(16, D, dtype=BF16)
@@ -873,7 +877,7 @@
         (info, u, cot, y_cls, *pieces1, *pieces0[3::4]),
         [SMEM, VMEM, VMEM, VMEM] + [ANY] * 40,
         (low, struct(TOK, D), row, low, low, low, low, low, struct(HEADS, TOK, TOK), struct(1536, D, dtype=BF16)) + (part,) * 4,
-        (VMEM,) * 8 + (ANY,) * 6,
+        (VMEM,) * 3 + (ANY,) * 11,
         weights
         + [
             pltpu.VMEM((GRANS * GRAN, D), BF16),
@@ -887,8 +891,9 @@
             mid, mid,
             pltpu.VMEM((8, GRAN, D), F32),
             mid16,
+            mid16, mid16, mid16, mid16, mid16,
             pltpu.SemaphoreType.DMA((64,)),
-            pltpu.SemaphoreType.DMA((30,)),
+            pltpu.SemaphoreType.DMA((35,)),
         ],
         flops=4 * TOK * PL,
         moved=4 * PL,
@@ -1020,11 +1025,11 @@
     *new, new_vecs, new_vecs_m, new_vecs_v, norm = pl.pallas_call(
         adamw_kernel,
         grid=(4,),
-        in_specs=[tile] + [block] * 4 + [small] * 4,
+        in_specs=[tile] * 4 + [block] * 4 + [small] * 4,
         out_specs=(block,) * 3 + (small,) * 3 + (SMEM,),
         out_shape=(struct(3456, 128),) * 3 + (struct(*vecs.shape),) * 3 + (struct(1, 1),),
         name="adamw",
-    )(sum_quick(square), flat, flat_view(mats_m), flat_view(mats_v), grads, vecs, vecs_m, vecs_v, grad_vecs)
+    )(*sum_quick(square), flat, flat_view(mats_m), flat_view(mats_v), grads, vecs, vecs_m, vecs_v, grad_vecs)
     new_mats, new_mats_m, new_mats_v = [flat_back(a) for a in new]
     return (
         head_out[None],

time: 341 us -> 339 us (level)
  waiting for transfers between devices: 160 us -> 166 us
  starting transfers between devices: 59.1 us -> 55.4 us
    ppermute x64, waiting for transfers between devices: 142 us -> 147 us  [flip(): lax.ppermute(v, axis, [(i, i ^ bit) for i in range(lax.axis_size(axis))])]
  transfers between devices with their start and end apart: 78 -> 78, of which waited for: 41 -> 44; matrix products, arithmetic and copies ran while one was open for 4% -> 3% of each run, Pallas kernels for 24% -> 23%
where the time goes in v2:
time: 339 us; the launch traced here: 336 us
  waiting for transfers between devices  166 us (49%)
  Pallas kernels  91.2 us (27%)
  starting transfers between devices  55.4 us (16%)
  other arithmetic  13.3 us (4%)
  local copies, waits for them, and re-layouts  8.5 us (3%)
    ppermute x64, waiting for transfers between devices, flip(): lax.ppermute(v, axis, [(i, i ^ bit) for i in range(lax.axis_size(axis))])  147 us
    pallas_call x7, Pallas kernels, call(): pl.pallas_call(kernel, out_shape=outs, in_specs=in_specs, out_specs=out_s...  77.2 us
    ppermute x64, starting transfers between devices, flip(): lax.ppermute(v, axis, [(i, i ^ bit) for i in range(lax.axis_size(axis))])  41.7 us
    ppermute x7, waiting for transfers between devices, z_up(): return lax.ppermute(v, 'dp', [(i, (i + 4) % n) for i in range(n)])  15.6 us
    convert_element_type x4, other arithmetic, add16(): return (a.astype(F32) + b.astype(F32)).astype(BF16)  6.78 us
  transfers between devices with their start and end apart: 78, of which 44 were waited for; matrix products, arithmetic and copies ran while one was open for 3% of the time, Pallas kernels for 23%

profile of v2, /device:TPU:0, one launch (start us, length us, event | category | flops | bytes accessed | tf_op | source)
XLA Modules:
  0.0 335.8 jit_solution(8345440313291333270)
XLA Ops:
  9.7 16.9 %collective-permute-done.refs_1_ = bf16[592,768]{1,0:T(8,128)(2,1)S(1)} collective-permute-done((bf16[592,768]{1,0:T(8,128)(2,1)}, bf16[592,768]{1,0:T(8,128)(2,1)S(1)}, u32[]{:S(2)}, u32[]{:S(2)}) %collective-permute-start) | collective-permute-done | bytes 909344 | tf_op jit(solution)/shard_map/ppermute | solution.py:98
  28.1 3.1 collective-permute-done.2.refs_4_
  35.6 25.7 %collective-permute-done.4.refs_3_ = bf16[288,768]{1,0:T(8,128)(2,1)} collective-permute-done((bf16[288,768]{1,0:T(8,128)(2,1)S(1)}, bf16[288,768]{1,0:T(8,128)(2,1)}, u32[]{:S(2)}, u32[]{:S(2)}) %collective-permute-start.4) | collective-permute-done | bytes 442400 | tf_op jit(solution)/shard_map/ppermute | solution.py:98
  66.8 8.6 %collective-permute-done.9.refs_7_ = bf16[288,768]{1,0:T(8,128)(2,1)} collective-permute-done((bf16[288,768]{1,0:T(8,128)(2,1)S(1)}, bf16[288,768]{1,0:T(8,128)(2,1)}, u32[]{:S(2)}, u32[]{:S(2)}) %collective-permute-start.9) | collective-permute-done | bytes 442400 | tf_op jit(solution)/shard_map/ppermute | solution.py:98
  77.4 13.7 %collective-permute-done.10.refs_9_ = bf16[592,768]{1,0:T(8,128)(2,1)S(1)} collective-permute-done((bf16[592,768]{1,0:T(8,128)(2,1)S(1)}, bf16[592,768]{1,0:T(8,128)(2,1)S(1)}, u32[]{:S(2)}, u32[]{:S(2)}) %collective-permute-start.10) | collective-permute-done | bytes 909344 | tf_op jit(solution)/shard_map/ppermute | solution.py:98
  96.0 17.7 %collective-permute-done.13.refs_13_ = bf16[592,768]{1,0:T(8,128)(2,1)S(1)} collective-permute-done((bf16[592,768]{1,0:T(8,128)(2,1)S(1)}, bf16[592,768]{1,0:T(8,128)(2,1)S(1)}, u32[]{:S(2)}, u32[]{:S(2)}) %collective-permute-start.13) | collective-permute-done | bytes 909344 | tf_op jit(solution)/shard_map/ppermute | solution.py:98
  113.7 3.3 collective-permute-done.14.refs_14_
  121.8 11.0 %collective-permute-done.20.refs_15_ = bf16[288,768]{1,0:T(8,128)(2,1)} collective-permute-done((bf16[288,768]{1,0:T(8,128)(2,1)S(1)}, bf16[288,768]{1,0:T(8,128)(2,1)}, u32[]{:S(2)}, u32[]{:S(2)}) %collective-permute-start.20) | collective-permute-done | bytes 442400 | tf_op jit(solution)/shard_map/ppermute | solution.py:98
  142.0 9.7 %first_forward.1 = (f32[16,768]{1,0:T(8,128)}, bf16[2,768]{1,0:T(2,128)(2,1)}, f32[16,768]{1,0:T(8,128)}, f32[16,128]{1,0:T(8,128)}, f32[16,768]{1,0:T(8,128)}, ...) custom-call(s32[8]{0:T(128)} %stack.23.info, ...), custom_call_target="tpu_custom_call" | custom-call | flops 452984832 | bytes 14155776 | tf_op jit(solution)/shard_map/first_forward/pallas_call | solution.py:815
  153.9 23.0 %second_block.1 = (bf16[256,768]{1,0:T(8,128)(2,1)}, f32[256,768]{1,0:T(8,128)}, f32[16,768]{1,0:T(8,128)}, bf16[256,768]{1,0:T(8,128)(2,1)}, bf16[256,768]{1,0:...) custom-call(s32[8]{0:T(128)} %stack.23.info, ...), custom_call_target="tpu_custom_call" | custom-call | flops 7247757312 | bytes 28311552 | tf_op jit(solution)/shard_map/second_block/pallas_call | solution.py:815
  188.9 14.2 %second_attention.1 = (f32[256,768]{1,0:T(8,128)}, f32[16,768]{1,0:T(8,128)}, bf16[1152,768]{1,0:T(8,128)(2,1)}, bf16[1152,768]{1,0:T(8,128)(2,1)}, bf16[1152,76...) custom-call(s32[8]{0:T(128)} %stack.23.info, f32[256,768]{1,0:T(8,128)} %get-tuple-element.165.dr, ...), custom_call_target="tpu_custom_call" | custom-call | flops 3623878656 | bytes 14155776 | tf_op jit(solution)/shard_map/second_attention/pallas_call | solution.py:815
  203.2 4.7 %collective-permute-done.45.over_y = bf16[576,768]{1,0:T(8,128)(2,1)} collective-permute-done((bf16[576,768]{1,0:T(8,128)(2,1)}, bf16[576,768]{1,0:T(8,128)(2,1)}, u32[]{:S(2)}, u32[]{:S(2)}) %collective-permute-start.45) | collective-permute-done | bytes 884768 | tf_op jit(solution)/shard_map/ppermute | solution.py:98
  212.2 3.7 %collective-permute-done.48 = bf16[1152,768]{1,0:T(8,128)(2,1)S(1)} collective-permute-done((bf16[1152,768]{1,0:T(8,128)(2,1)S(1)}, bf16[1152,768]{1,0:T(8,128)(2,1)S(1)}, u32[]{:S(2)}, u32[]{:S(2)}) %collective-permute-start.48) | collective-permute-done | bytes 1769504 | tf_op jit(solution)/shard_map/ppermute | solution.py:98
  220.3 4.4 %collective-permute-done.47 = bf16[32,768]{1,0:T(8,128)(2,1)S(1)} collective-permute-done((bf16[32,768]{1,0:T(8,128)(2,1)S(1)}, bf16[32,768]{1,0:T(8,128)(2,1)S(1)}, u32[]{:S(2)}, u32[]{:S(2)}) %collective-permute-start.47) | collective-permute-done | bytes 49184 | tf_op jit(solution)/shard_map/ppermute | solution.py:98
  226.0 14.4 %first_backward.1 = (f32[256,768]{1,0:T(8,128)}, bf16[96,768]{1,0:T(8,128)(2,1)}, f32[1,1]{1,0:T(1,128)}) custom-call(s32[8]{0:T(128)} %stack.23.info, bf16[256,768]{1,0:T(8,128)(2,1)} %bitcast.47, bf16[64,768]{1,0:T(8,128)(2,1)} %pad_maximum_fusion.cls_all, f32[256,768]{1,0:T(8,128)} %get-tuple-element.182.dz, f32[16,768]{1,0:T(8,128)} %get-tuple-element.183.vg1, ...), custom_call_target="tpu_custom_call" | custom-call | flops 452984832 | bytes 14155776 | tf_op jit(solution)/shard_map/first_backward/pallas_call | solution.py:815
  243.1 6.5 %collective-permute-done.52.last_x = bf16[288,768]{1,0:T(8,128)(2,1)S(1)} collective-permute-done((bf16[288,768]{1,0:T(8,128)(2,1)}, bf16[288,768]{1,0:T(8,128)(2,1)S(1)}, u32[]{:S(2)}, u32[]{:S(2)}) %collective-permute-start.52) | collective-permute-done | bytes 442400 | tf_op jit(solution)/shard_map/ppermute | solution.py:98
  255.6 3.1 total.1
  262.4 4.3 %order.1 = (bf16[288,768]{1,0:T(8,128)(2,1)}, bf16[288,768]{1,0:T(8,128)(2,1)}, bf16[288,768]{1,0:T(8,128)(2,1)}, bf16[288,768]{1,0:T(8,128)(2,1)}) custom-call(s32[8]{0:T(128)} %stack.23.info, bf16[288,768]{1,0:T(8,128)(2,1)} %get-tuple-element.210.a3, bf16[288,768]{1,0:T(8,128)(2,1)} %get-tuple-element.211.a2, bf16[1152,768]{1,0:T(8,128)(2,1)} %get-tuple-element.199.mine, ...), custom_call_target="tpu_custom_call" | custom-call | tf_op jit(solution)/shard_map/order/pallas_call | solution.py:979
  270.6 8.4 %collective-permute-done.68 = bf16[288,768]{1,0:T(8,128)(2,1)S(1)} collective-permute-done((bf16[288,768]{1,0:T(8,128)(2,1)}, bf16[288,768]{1,0:T(8,128)(2,1)S(1)}, u32[]{:S(2)}, u32[]{:S(2)}) %collective-permute-start.68) | collective-permute-done | bytes 442400 | tf_op jit(solution)/shard_map/ppermute | solution.py:115
  285.0 3.9 %collective-permute-done.59.refs_3_ = bf16[192,768]{1,0:T(8,128)(2,1)} collective-permute-done((bf16[192,768]{1,0:T(8,128)(2,1)S(1)}, bf16[192,768]{1,0:T(8,128)(2,1)}, u32[]{:S(2)}, u32[]{:S(2)}) %collective-permute-start.59) | collective-permute-done | bytes 294944 | tf_op jit(solution)/shard_map/ppermute | solution.py:98
  288.9 3.9 %collective-permute-done.60.refs_4_ = bf16[192,768]{1,0:T(8,128)(2,1)} collective-permute-done((bf16[192,768]{1,0:T(8,128)(2,1)S(1)}, bf16[192,768]{1,0:T(8,128)(2,1)}, u32[]{:S(2)}, u32[]{:S(2)}) %collective-permute-start.60) | collective-permute-done | bytes 294944 | tf_op jit(solution)/shard_map/ppermute | solution.py:98
  296.0 10.1 %owner_grad.1 = (f32[1728,128]{1,0:T(8,128)}, f32[24,768]{1,0:T(8,128)}) custom-call(s32[8]{0:T(128)} %stack.23.info, bf16[384,768]{1,0:T(8,128)(2,1)} %copy-done.34, bf16[384,768]{1,0:T(8,128)(2,1)} %copy-done.32, bf16[384,768]{1,0:T(8,128)(2,1)} %copy-done.33, bf16[192,768]{1,0:T(8,128)(2,1)} %collective-permute-done.59.refs_3_, ...), custom_call_target="tpu_custom_call" | custom-call | flops 905969664 | bytes 4718592 | tf_op jit(solution)/shard_map/owner_grad/pallas_call | solution.py:815
  308.4 3.2 join_grads.1
  328.8 6.6 %adamw.1 = (f32[3456,128]{1,0:T(8,128)}, f32[3456,128]{1,0:T(8,128)}, f32[3456,128]{1,0:T(8,128)}, f32[2,288]{1,0:T(2,128)}, f32[2,288]{1,0:T(2,128)}, /*index=5*/f32[2,288]{1,0:T(2,128)}, f32[1,1]{1,0:T(1,128)}) custom-call(f32[8,128]{1,0:T(8,128)} %copy-done.42, f32[8,128]{1,0:T(8,128)} %copy-done.43, f32[8,128]{1,0:T(8,128)} %copy-done.44, ...), custom_call_target="tpu_custom_call" | custom-call | tf_op jit(solution)/shard_map/adamw/pallas_call | solution.py:1025
  (270 shorter events, 110.1 us)
Async XLA Ops:
  3.3 23.4 %collective-permute-start = (bf16[592,768]{1,0:T(8,128)(2,1)}, bf16[592,768]{1,0:T(8,128)(2,1)S(1)}, u32[]{:S(2)}, u32[]{:S(2)}) collective-permute-start(bf16[592,768]{1,0:T(8,128)(2,1)} %pack.1.refs_0_), channel_id=1, source_target_pairs={{0,4},{2,6},{4,0},{6,2},{8,12},{10,14},{12,8},{14,10},{16,20},{18,... | collective-permute-start | bytes 2727944 | tf_op jit(solution)/shard_map/ppermute | solution.py:98
  6.2 21.8 %collective-permute-start.1 = (bf16[592,768]{1,0:T(8,128)(2,1)}, bf16[592,768]{1,0:T(8,128)(2,1)S(1)}, u32[]{:S(2)}, u32[]{:S(2)}) collective-permute-start(bf16[592,768]{1,0:T(8,128)(2,1)} %pack.1.refs_0_), channel_id=1, source_target_pairs={{0,1},{1,0},{2,3},{3,2},{4,5},{5,4},{6,7},{7,6},{8,9},{9,8},{10,11... | collective-permute-start | bytes 2727944 | tf_op jit(solution)/shard_map/ppermute | solution.py:98
  7.8 23.5 %collective-permute-start.2 = (bf16[592,768]{1,0:T(8,128)(2,1)}, bf16[592,768]{1,0:T(8,128)(2,1)S(1)}, u32[]{:S(2)}, u32[]{:S(2)}) collective-permute-start(bf16[592,768]{1,0:T(8,128)(2,1)} %pack.1.refs_0_), channel_id=1, source_target_pairs={{0,8},{2,10},{4,12},{6,14},{8,16},{10,18},{12,20},{14,22},{16,24},... | collective-permute-start | bytes 2727944 | tf_op jit(solution)/shard_map/ppermute | solution.py:115
  31.2 30.8 %collective-permute-start.5 = (bf16[592,768]{1,0:T(8,128)(2,1)S(1)}, bf16[592,768]{1,0:T(8,128)(2,1)S(1)}, u32[]{:S(2)}, u32[]{:S(2)}) collective-permute-start(bf16[592,768]{1,0:T(8,128)(2,1)S(1)} %collective-permute-done.2.refs_4_), channel_id=1, source_target_pairs={{0,4},{2,6},{4,0},{6,2},{8,12},{10,14},{12,8},{14,10},{16,20},{18,... | collective-permute-start | bytes 2727944 | tf_op jit(solution)/shard_map/ppermute | solution.py:98
  31.7 30.3 %collective-permute-start.6 = (bf16[592,768]{1,0:T(8,128)(2,1)S(1)}, bf16[592,768]{1,0:T(8,128)(2,1)S(1)}, u32[]{:S(2)}, u32[]{:S(2)}) collective-permute-start(bf16[592,768]{1,0:T(8,128)(2,1)S(1)} %collective-permute-done.2.refs_4_), channel_id=1, source_target_pairs={{0,1},{1,0},{2,3},{3,2},{4,5},{5,4},{6,7},{7,6},{8,9},{9,8},{10,11... | collective-permute-start | bytes 2727944 | tf_op jit(solution)/shard_map/ppermute | solution.py:98
  32.2 29.8 %collective-permute-start.7 = (bf16[592,768]{1,0:T(8,128)(2,1)S(1)}, bf16[592,768]{1,0:T(8,128)(2,1)S(1)}, u32[]{:S(2)}, u32[]{:S(2)}) collective-permute-start(bf16[592,768]{1,0:T(8,128)(2,1)S(1)} %collective-permute-done.2.refs_4_), channel_id=1, source_target_pairs={{0,8},{2,10},{4,12},{6,14},{8,16},{10,18},{12,20},{14,22},{16,24},... | collective-permute-start | bytes 2727944 | tf_op jit(solution)/shard_map/ppermute | solution.py:115
  32.3 29.7 %collective-permute-start.3 = (bf16[304,768]{1,0:T(8,128)(2,1)S(1)}, bf16[304,768]{1,0:T(8,128)(2,1)S(1)}, u32[]{:S(2)}, u32[]{:S(2)}) collective-permute-start(bf16[304,768]{1,0:T(8,128)(2,1)S(1)} %slice.88), channel_id=1, source_target_pairs={{0,1},{1,0},{2,3},{3,2},{4,5},{5,4},{6,7},{7,6},{8,9},{9,8},{10,11... | collective-permute-start | bytes 1400840 | tf_op jit(solution)/shard_map/ppermute | solution.py:98
  34.0 27.3 %collective-permute-start.4 = (bf16[288,768]{1,0:T(8,128)(2,1)S(1)}, bf16[288,768]{1,0:T(8,128)(2,1)}, u32[]{:S(2)}, u32[]{:S(2)}) collective-permute-start(bf16[288,768]{1,0:T(8,128)(2,1)S(1)} %slice.89), channel_id=1, source_target_pairs={{0,4},{2,6},{4,0},{6,2},{8,12},{10,14},{12,8},{14,10},{16,20},{18,... | collective-permute-start | bytes 1327112 | tf_op jit(solution)/shard_map/ppermute | solution.py:98
  64.2 26.8 %collective-permute-start.10 = (bf16[592,768]{1,0:T(8,128)(2,1)S(1)}, bf16[592,768]{1,0:T(8,128)(2,1)S(1)}, u32[]{:S(2)}, u32[]{:S(2)}) collective-permute-start(bf16[592,768]{1,0:T(8,128)(2,1)S(1)} %collective-permute-done.7.refs_8_), channel_id=1, source_target_pairs={{0,4},{2,6},{4,0},{6,2},{8,12},{10,14},{12,8},{14,10},{16,20},{18,... | collective-permute-start | bytes 2727944 | tf_op jit(solution)/shard_map/ppermute | solution.py:98
  65.0 26.1 %collective-permute-start.11 = (bf16[592,768]{1,0:T(8,128)(2,1)S(1)}, bf16[592,768]{1,0:T(8,128)(2,1)S(1)}, u32[]{:S(2)}, u32[]{:S(2)}) collective-permute-start(bf16[592,768]{1,0:T(8,128)(2,1)S(1)} %collective-permute-done.7.refs_8_), channel_id=1, source_target_pairs={{0,8},{2,10},{4,12},{6,14},{8,16},{10,18},{12,20},{14,22},{16,24},... | collective-permute-start | bytes 2727944 | tf_op jit(solution)/shard_map/ppermute | solution.py:115
  65.4 27.5 %collective-permute-start.12 = (bf16[592,768]{1,0:T(8,128)(2,1)S(1)}, bf16[592,768]{1,0:T(8,128)(2,1)S(1)}, u32[]{:S(2)}, u32[]{:S(2)}) collective-permute-start(bf16[592,768]{1,0:T(8,128)(2,1)S(1)} %collective-permute-done.7.refs_8_), channel_id=1, source_target_pairs={{0,1},{1,0},{2,3},{3,2},{4,5},{5,4},{6,7},{7,6},{8,9},{9,8},{10,11... | collective-permute-start | bytes 2727944 | tf_op jit(solution)/shard_map/ppermute | solution.py:98
  93.4 23.6 %collective-permute-start.14 = (bf16[592,768]{1,0:T(8,128)(2,1)S(1)}, bf16[592,768]{1,0:T(8,128)(2,1)S(1)}, u32[]{:S(2)}, u32[]{:S(2)}) collective-permute-start(bf16[592,768]{1,0:T(8,128)(2,1)S(1)} %collective-permute-done.12.refs_10_), channel_id=1, source_target_pairs={{0,8},{2,10},{4,12},{6,14},{8,16},{10,18},{12,20},{14,22},{16,24},... | collective-permute-start | bytes 2727944 | tf_op jit(solution)/shard_map/ppermute | solution.py:115
  94.5 22.5 %collective-permute-start.15 = (bf16[592,768]{1,0:T(8,128)(2,1)S(1)}, bf16[592,768]{1,0:T(8,128)(2,1)S(1)}, u32[]{:S(2)}, u32[]{:S(2)}) collective-permute-start(bf16[592,768]{1,0:T(8,128)(2,1)S(1)} %collective-permute-done.10.refs_9_), channel_id=1, source_target_pairs={{0,1},{1,0},{2,3},{3,2},{4,5},{5,4},{6,7},{7,6},{8,9},{9,8},{10,11... | collective-permute-start | bytes 2727944 | tf_op jit(solution)/shard_map/ppermute | solution.py:98
  95.5 22.0 %collective-permute-start.25 = (bf16[592,768]{1,0:T(8,128)(2,1)S(1)}, bf16[592,768]{1,0:T(8,128)(2,1)S(1)}, u32[]{:S(2)}, u32[]{:S(2)}) collective-permute-start(bf16[592,768]{1,0:T(8,128)(2,1)S(1)} %collective-permute-done.2.refs_4_), channel_id=1, source_target_pairs={{0,2},{2,0},{4,6},{6,4},{8,10},{10,8},{12,14},{14,12},{16,18},{18,... | collective-permute-start | bytes 2727944 | tf_op jit(solution)/shard_map/ppermute | solution.py:98
  95.6 25.1 %collective-permute-start.26 = (bf16[592,768]{1,0:T(8,128)(2,1)S(1)}, bf16[592,768]{1,0:T(8,128)(2,1)S(1)}, u32[]{:S(2)}, u32[]{:S(2)}) collective-permute-start(bf16[592,768]{1,0:T(8,128)(2,1)S(1)} %collective-permute-done.5.refs_5_), channel_id=1, source_target_pairs={{0,2},{2,0},{4,6},{6,4},{8,10},{10,8},{12,14},{14,12},{16,18},{18,... | collective-permute-start | bytes 2727944 | tf_op jit(solution)/shard_map/ppermute | solution.py:98
  151.7 25.2 %collective-permute-start.37 = (bf16[2,768]{1,0:T(2,128)(2,1)}, bf16[2,768]{1,0:T(2,128)(2,1)S(1)}, u32[]{:S(2)}, u32[]{:S(2)}) collective-permute-start(bf16[2,768]{1,0:T(2,128)(2,1)} %get-tuple-element.157), channel_id=1, source_target_pairs={{0,1},{1,0},{2,3},{3,2},{4,5},{5,4},{6,7},{7,6},{8,9},{9,8},{10,11... | collective-permute-start | bytes 9224 | tf_op jit(solution)/shard_map/ppermute | solution.py:127
  153.3 23.6 %collective-permute-start.38 = (bf16[2,768]{1,0:T(2,128)(2,1)}, bf16[2,768]{1,0:T(2,128)(2,1)S(1)}, u32[]{:S(2)}, u32[]{:S(2)}) collective-permute-start(bf16[2,768]{1,0:T(2,128)(2,1)} %get-tuple-element.157), channel_id=1, source_target_pairs={{0,2},{2,0},{4,6},{6,4},{8,10},{10,8},{12,14},{14,12},{16,18},{18,... | collective-permute-start | bytes 9224 | tf_op jit(solution)/shard_map/ppermute | solution.py:98
  153.3 23.7 %collective-permute-start.39 = (bf16[2,768]{1,0:T(2,128)(2,1)}, bf16[2,768]{1,0:T(2,128)(2,1)S(1)}, u32[]{:S(2)}, u32[]{:S(2)}) collective-permute-start(bf16[2,768]{1,0:T(2,128)(2,1)} %get-tuple-element.157), channel_id=1, source_target_pairs={{0,3},{1,2},{2,1},{3,0},{4,7},{5,6},{6,5},{7,4},{8,11},{9,10},{10,... | collective-permute-start | bytes 9224 | tf_op jit(solution)/shard_map/ppermute | solution.py:127
  177.1 26.1 %collective-permute-start.40 = (bf16[1152,768]{1,0:T(8,128)(2,1)}, bf16[1152,768]{1,0:T(8,128)(2,1)}, u32[]{:S(2)}, u32[]{:S(2)}) collective-permute-start(bf16[1152,768]{1,0:T(8,128)(2,1)} %get-tuple-element.158), channel_id=1, source_target_pairs={{0,2},{2,0},{4,6},{6,4},{8,10},{10,8},{12,14},{14,12},{16,18},{18,... | collective-permute-start | bytes 5308424 | tf_op jit(solution)/shard_map/ppermute | solution.py:98
  217.6 23.5 %collective-permute-start.49 = (bf16[1152,768]{1,0:T(8,128)(2,1)}, bf16[1152,768]{1,0:T(8,128)(2,1)}, u32[]{:S(2)}, u32[]{:S(2)}) collective-permute-start(bf16[1152,768]{1,0:T(8,128)(2,1)} %get-tuple-element.200), channel_id=1, source_target_pairs={{0,2},{2,0},{4,6},{6,4},{8,10},{10,8},{12,14},{14,12},{16,18},{18,... | collective-permute-start | bytes 5308424 | tf_op jit(solution)/shard_map/ppermute | solution.py:98
  217.7 22.8 %collective-permute-start.50 = (bf16[576,768]{1,0:T(8,128)(2,1)}, bf16[576,768]{1,0:T(8,128)(2,1)}, u32[]{:S(2)}, u32[]{:S(2)}) collective-permute-start(bf16[576,768]{1,0:T(8,128)(2,1)} %get-tuple-element.201), channel_id=1, source_target_pairs={{0,1},{1,0},{2,3},{3,2},{4,5},{5,4},{6,7},{7,6},{8,9},{9,8},{10,11... | collective-permute-start | bytes 2654216 | tf_op jit(solution)/shard_map/ppermute | solution.py:98
  218.2 22.8 %collective-permute-start.51 = (bf16[576,768]{1,0:T(8,128)(2,1)}, bf16[576,768]{1,0:T(8,128)(2,1)}, u32[]{:S(2)}, u32[]{:S(2)}) collective-permute-start(bf16[576,768]{1,0:T(8,128)(2,1)} %get-tuple-element.202), channel_id=1, source_target_pairs={{0,4},{2,6},{4,0},{6,2},{8,12},{10,14},{12,8},{14,10},{16,20},{18,... | collective-permute-start | bytes 2654216 | tf_op jit(solution)/shard_map/ppermute | solution.py:98
  219.2 30.4 %collective-permute-start.52 = (bf16[288,768]{1,0:T(8,128)(2,1)}, bf16[288,768]{1,0:T(8,128)(2,1)S(1)}, u32[]{:S(2)}, u32[]{:S(2)}) collective-permute-start(bf16[288,768]{1,0:T(8,128)(2,1)} %get-tuple-element.204), channel_id=1, source_target_pairs={{0,4},{2,6},{4,0},{6,2},{8,12},{10,14},{12,8},{14,10},{16,20},{18,... | collective-permute-start | bytes 1327112 | tf_op jit(solution)/shard_map/ppermute | solution.py:98
  224.7 24.9 %collective-permute-start.53 = (bf16[288,768]{1,0:T(8,128)(2,1)}, bf16[288,768]{1,0:T(8,128)(2,1)}, u32[]{:S(2)}, u32[]{:S(2)}) collective-permute-start(bf16[288,768]{1,0:T(8,128)(2,1)} %get-tuple-element.205), channel_id=1, source_target_pairs={{0,1},{1,0},{2,3},{3,2},{4,5},{5,4},{6,7},{7,6},{8,9},{9,8},{10,11... | collective-permute-start | bytes 1327112 | tf_op jit(solution)/shard_map/ppermute | solution.py:98
  (103 other events, 1751.4 us)
